TPU v7x, 128 devices: a whole 4x4x4 slice. The times are simulated.
128 devices in a mesh: section: 4 (over z), tensor: 16 (over x_lo, y, core), dp: 2 (over x_hi).
Axes of the slice: x: 4 (x_hi: 2, x_lo: 2; x = x_hi * 2 + x_lo), y: 4, z: 4, core: 2. Of those that a mesh axis runs over, the one named last changes fastest.
Arguments:
- x_in: bfloat16 [4, 5376, 256], P('section', 'tensor', 'dp'), may hold values from -6 to 6
- final_hidden: bfloat16 [5376, 256], P('tensor', 'dp'), may hold values from -6.8 to 6.8
- w_up: bfloat16 [4, 5376, 21504], P('section', None, ('tensor', 'dp')), may hold values from -0.078125 to 0.078125
- w_down: bfloat16 [4, 21504, 5376], P('section', ('tensor', 'dp')), may hold values from -0.0390625 to 0.0390625
- table: bfloat16 [131072, 5376], P(('section', 'tensor', 'dp')), may hold values from -1.2274756 to 1.2274756
- token_ids: int32 [256], replicated, may hold values from 0 to 131071
- targets: int32 [256], replicated, may hold values from 0 to 131071
- proj_in: bfloat16 [4, 64, 21504], P('section', None, ('tensor', 'dp')), may hold values from -0.0390625 to 0.0390625
- proj_out: bfloat16 [4, 64, 5376], P('section'), may hold values from -1.5 to 1.5
- proj_vocab: bfloat16 [64, 131072], P(None, ('section', 'tensor', 'dp')), may hold values from -1.796875 to 1.796875
- proj_dim: bfloat16 [64, 5376], P(None, 'tensor'), may hold values from -0.078125 to 0.078125
Outputs:
- layer_grads: float32 [4, 2, 64, 64], P('section', 'dp')
- table_grads: float32 [2, 64, 64], P('dp')
All inputs are finite; a program needn't handle non-finite values.
Results may differ from a plain program's by a relative error of at most 0.015.
Values may be sent and summed in bfloat16 or wider, within the bound.
A program may use at most 192 MiB of HBM per device.

v0:
```python
import math

import jax
import jax.numpy as jnp
from jax import lax
from jax.sharding import PartitionSpec as P

D = 5376
SEQ_LEN = 128


def from_behind(value, axis, steps):
    count = lax.axis_size(axis)
    first, last = (max(0, -steps), min(count, count - steps))
    return lax.ppermute(value, axis, [(source, source + steps) for source in range(first, last)])


def silu_slope(hidden):
    gate = jax.nn.sigmoid(hidden)
    return gate * (1.0 + hidden * (1.0 - gate))


def per_sequence(left, right):
    count = left.shape[0] // SEQ_LEN
    return jnp.einsum(
        "slr,slq->srq",
        left.reshape(count, SEQ_LEN, -1),
        right.reshape(count, SEQ_LEN, -1),
        precision=lax.Precision.HIGHEST,
    )


def contract(left, right, left_dim, right_dim):
    return lax.dot_general(
        left, right, (((left_dim,), (right_dim,)), ((), ())), preferred_element_type=jnp.float32
    )


def feature_fold(operand, update, initial):
    return update(initial, lax.all_gather(operand, "tensor", axis=0, tiled=True), jnp.int32(0))


def feature_sum(term_fn, shard_rows):
    return lax.psum_scatter(
        term_fn(jnp.int32(0), shard_rows * lax.axis_size("tensor")),
        "tensor",
        scatter_dimension=0,
        tiled=True,
    )


def vocab_sums(operand):
    return lax.psum(operand, ("section", "tensor", "dp"))


def pass_back(operand):
    return from_behind(operand, "section", -1)


def shards(
    x_in,
    final_hidden,
    w_up,
    w_down,
    table,
    token_ids,
    targets,
    proj_in,
    proj_out,
    proj_vocab,
    proj_dim,
):
    section_count = lax.axis_size("section")
    section_pos = lax.axis_index("section")
    replica = lax.axis_index("dp")
    replica_count = lax.axis_size("dp")
    shard_rows = x_in.shape[1]
    tok_rep = x_in.shape[2]
    vocab_dev = table.shape[0]
    rank_dim = proj_dim.shape[0]
    out_proj = proj_out[0]
    up_full, down_full, pin_full, hidden_pair = (
        lax.all_gather(w_up[0], "dp", axis=1, tiled=True),
        lax.all_gather(w_down[0], "dp", axis=0, tiled=True),
        lax.all_gather(proj_in[0], "dp", axis=1, tiled=True),
        lax.all_gather(final_hidden, "dp", axis=1, tiled=True),
    )
    x_rows = x_in[0]
    unit_count = up_full.shape[1]
    token_count = hidden_pair.shape[1]

    def up_step(running, portion, first_row):
        return contract(portion, up_full, 0, 0)

    hidden = feature_fold(x_rows, up_step, jnp.zeros((x_rows.shape[1], unit_count), jnp.float32))
    activated = jax.nn.silu(hidden).astype(jnp.bfloat16)
    slope = silu_slope(hidden)

    def logit_step(running, portion, first_row):
        return contract(portion, table, 0, 1)

    logits = feature_fold(hidden_pair, logit_step, jnp.zeros((token_count, vocab_dev), jnp.float32))
    dim_term = contract(hidden_pair, proj_dim, 0, 1)
    input_proj, dim_side = lax.psum((contract(activated, pin_full, 1, 1), dim_term), "tensor")
    local_peak = jnp.max(logits, axis=1)
    row_peak = lax.pmax(local_peak, ("section", "tensor", "dp"))
    row_total = vocab_sums(jnp.sum(jnp.exp(logits - row_peak[:, None]), axis=1))
    probability = jnp.exp(logits - row_peak[:, None]) / row_total[:, None]
    columns = lax.axis_index(("section", "tensor", "dp")) * vocab_dev + jnp.arange(
        vocab_dev, dtype=jnp.int32
    )
    target_hot = (targets[:, None] == columns[None, :]).astype(jnp.float32)
    logit_grad = (probability - target_hot).astype(jnp.bfloat16)
    token_hot = (token_ids[:, None] == columns[None, :]).astype(jnp.bfloat16)
    vocab_side, token_side = vocab_sums(
        (contract(logit_grad, proj_vocab, 1, 1), contract(token_hot, proj_vocab, 1, 1))
    )

    def head_term(offset, row_count):
        return contract(table, logit_grad, 0, 1)

    head_part = feature_sum(head_term, shard_rows)
    head_full = lax.psum(head_part, ("section", "dp"))
    head_cot = lax.dynamic_slice_in_dim(head_full, replica * tok_rep, tok_rep, 1).astype(
        jnp.bfloat16
    )
    proj_kept = jnp.zeros((tok_rep, rank_dim), jnp.float32)
    first_cot = jnp.zeros_like(head_cot)
    cotangent = head_cot
    for section_step in range(section_count):
        active = section_pos == section_count - 1 - section_step
        gathered = cotangent
        gather_len = gathered.shape[1]

        def down_step(running, portion, first_row):
            return (contract(portion, down_full, 0, 1), contract(portion, out_proj, 0, 1))

        initial = (
            jnp.zeros((gather_len, unit_count), jnp.float32),
            jnp.zeros((gather_len, rank_dim), jnp.float32),
        )
        act_grad, projected = feature_fold(gathered, down_step, initial)
        hidden_grad = (act_grad * slope).astype(jnp.bfloat16)

        def back_term(offset, row_count):
            return contract(up_full, hidden_grad, 1, 1)

        backflow = feature_sum(back_term, shard_rows)
        updated = (cotangent.astype(jnp.float32) + backflow).astype(jnp.bfloat16)
        updated, projected = (updated, projected)
        proj_kept = jnp.where(active, projected, proj_kept)
        if section_step + 1 < section_count:
            cotangent = pass_back(updated)
        else:
            first_cot = updated
    embed_part = math.sqrt(D) * contract(first_cot, proj_dim, 0, 1)
    embed_part = jnp.where(section_pos == 0, embed_part, jnp.zeros_like(embed_part))
    embed_slots = jnp.zeros((replica_count * tok_rep, rank_dim), jnp.float32)
    embed_slots = lax.dynamic_update_slice_in_dim(embed_slots, embed_part, replica * tok_rep, 0)
    embed_side = vocab_sums(embed_slots)
    own_start = replica * tok_rep
    own_vocab = lax.dynamic_slice_in_dim(vocab_side, own_start, tok_rep, 0)
    own_dim = lax.dynamic_slice_in_dim(dim_side, own_start, tok_rep, 0)
    own_token = lax.dynamic_slice_in_dim(token_side, own_start, tok_rep, 0)
    own_embed = lax.dynamic_slice_in_dim(embed_side, own_start, tok_rep, 0)
    table_grads = per_sequence(own_vocab, own_dim) + per_sequence(own_token, own_embed)
    layer_grads = per_sequence(proj_kept, input_proj)[None]
    return (layer_grads, table_grads)


def solution(mesh):
    placed = (
        P("section", "tensor", "dp"),
        P("tensor", "dp"),
        P("section", None, ("tensor", "dp")),
        P("section", ("tensor", "dp"), None),
        P(("section", "tensor", "dp"), None),
        P(),
        P(),
        P("section", None, ("tensor", "dp")),
        P("section", None, None),
        P(None, ("section", "tensor", "dp")),
        P(None, "tensor"),
    )
    return jax.shard_map(
        shards,
        mesh=mesh,
        in_specs=placed,
        out_specs=(P("section", "dp", None, None), P("dp", None, None)),
        check_vma=False,
    )
```

profile of v0, /device:TPU:32, one launch (start us, length us, event | category | flops | bytes accessed | tf_op | source)
XLA Modules:
  0.0 1437.1 jit_solution(1300356408957218516)
XLA Ops:
  7.2 8.2 all_gather.30
  15.6 36.2 %all-gather.13.cloned.1.call-done = bf16[5376,256]{1,0:T(8,128)(2,1)} async-done(((bf16[336,256]{1,0:T(8,128)(2,1)}), bf16[5376,256]{1,0:T(8,128)(2,1)}) %all-gather.13.cloned.1.call-update) | async-done | bytes 2752528 | tf_op jit(solution)/shard_map/all_gather | solution.py:40
  58.6 64.3 %pmax.7 = f32[256]{0:T(256)S(1)} all-reduce(f32[256]{0:T(256)S(1)} %get-tuple-element.5), channel_id=1, replica_groups=mesh['section'=4,'tensor'=16,'dp'=2] {'section','tensor','dp'}, use_global_device_ids=true, to_apply=%region_1.2 | all-reduce | flops 256 | bytes 2048 | tf_op jit(solution)/shard_map/pmax | solution.py:106
  123.3 62.7 %psum.49 = f32[256]{0:T(256)S(1)} all-reduce(f32[256]{0:T(256)S(1)} %fusion.68), channel_id=1, replica_groups=mesh['section'=4,'tensor'=16,'dp'=2] {'section','tensor','dp'}, use_global_device_ids=true, to_apply=%region_3.4 | all-reduce | flops 256 | bytes 2048 | tf_op jit(solution)/shard_map/psum | solution.py:53
  186.3 9.0 convolution_bitcast_fusion
  203.3 65.5 %reduce-scatter.16.cloned.1.call-done = f32[336,256]{1,0:T(8,128)} async-done(((f32[5376,256]{1,0:T(8,128)}), f32[336,256]{1,0:T(8,128)}) %reduce-scatter.16.cloned.1.call-update) | async-done | bytes 344080
  270.0 47.4 %all-reduce.8 = bf16[336,256]{0,1:T(8,128)(2,1)S(1)} all-reduce(f32[336,256]{0,1:T(8,128)S(1)} %copy.25), channel_id=1, replica_groups=mesh['section'=4,'tensor'=16,'dp'=2] {'section','dp'}, use_global_device_ids=true, to_apply=%region_5.6 | all-reduce | flops 86016 | bytes 516096 | tf_op jit(solution)/shard_map/psum | solution.py:123
  318.7 162.6 %all-gather.27.cloned.1.call-done = bf16[1,5376,1344]{1,2,0:T(8,128)(2,1)} async-done(((bf16[1,5376,672]{1,2,0:T(8,128)(2,1)}), bf16[1,5376,1344]{1,2,0:T(8,128)(2,1)}) %all-gather.27.cloned.1.call-update) | async-done | bytes 14450704 | tf_op jit(solution)/shard_map/all_gather | solution.py:83
  488.9 170.6 %all-gather.23.cloned.1.call-done = bf16[1,1344,5376]{2,1,0:T(8,128)(2,1)} async-done(((bf16[1,672,5376]{2,1,0:T(8,128)(2,1)}), bf16[1,1344,5376]{2,1,0:T(8,128)(2,1)}) %all-gather.23.cloned.1.call-update) | async-done | bytes 14450704 | tf_op jit(solution)/shard_map/all_gather | solution.py:84
  659.5 34.2 %all-gather.15.cloned.1.call-done = bf16[5376,128]{1,0:T(8,128)(2,1)} async-done(((bf16[336,128]{1,0:T(8,128)(2,1)}), bf16[5376,128]{1,0:T(8,128)(2,1)}) %all-gather.15.cloned.1.call-update) | async-done | bytes 1376272 | tf_op jit(solution)/shard_map/all_gather | solution.py:40
  693.6 21.4 %fusion.18 = f32[5376,128]{0,1:T(8,128)} fusion(bf16[1,5376,1344]{1,2,0:T(8,128)(2,1)} %all-gather.27.cloned.1.call-done, bf16[5376,128]{1,0:T(8,128)(2,1)} %all-gather.15.cloned.1.call-done, bf16[1,1344,5376]{2,1,0:T(8,128)(2,1)} %all-gather.23.cloned.1.call-done, f32[128,1344]{0,1:T(8,128)S(1)} %fusion.8), kind=kOutput, calls=%fused_computation.19 | convolution fusion | flops 3700924416 | bytes 33718272 | tf_op jit(solution)/shard_map/dot_general | solution.py:34
  718.4 64.4 %reduce-scatter.18.cloned.1.call-done = f32[336,128]{1,0:T(8,128)} async-done(((f32[5376,128]{1,0:T(8,128)}), f32[336,128]{1,0:T(8,128)}) %reduce-scatter.18.cloned.1.call-update) | async-done | bytes 172048
  791.4 31.5 %all-gather.17.cloned.1.call-done = bf16[5376,128]{1,0:T(8,128)(2,1)} async-done(((bf16[336,128]{1,0:T(8,128)(2,1)}), bf16[5376,128]{1,0:T(8,128)(2,1)}) %all-gather.17.cloned.1.call-update) | async-done | bytes 1376272 | tf_op jit(solution)/shard_map/all_gather | solution.py:40
  822.9 21.4 %fusion.21 = f32[5376,128]{0,1:T(8,128)} fusion(bf16[1,5376,1344]{1,2,0:T(8,128)(2,1)} %all-gather.27.cloned.1.call-done, bf16[5376,128]{1,0:T(8,128)(2,1)} %all-gather.17.cloned.1.call-done, bf16[1,1344,5376]{2,1,0:T(8,128)(2,1)} %all-gather.23.cloned.1.call-done, f32[128,1344]{0,1:T(8,128)S(1)} %fusion.8), kind=kOutput, calls=%fused_computation.20 | convolution fusion | flops 3700924416 | bytes 33718272 | tf_op jit(solution)/shard_map/dot_general | solution.py:34
  847.6 64.5 %reduce-scatter.20.cloned.1.call-done = f32[336,128]{1,0:T(8,128)} async-done(((f32[5376,128]{1,0:T(8,128)}), f32[336,128]{1,0:T(8,128)}) %reduce-scatter.20.cloned.1.call-update) | async-done | bytes 172048
  920.7 31.4 %all-gather.19.cloned.1.call-done = bf16[5376,128]{1,0:T(8,128)(2,1)} async-done(((bf16[336,128]{1,0:T(8,128)(2,1)}), bf16[5376,128]{1,0:T(8,128)(2,1)}) %all-gather.19.cloned.1.call-update) | async-done | bytes 1376272 | tf_op jit(solution)/shard_map/all_gather | solution.py:40
  952.1 21.4 %fusion.24 = f32[5376,128]{0,1:T(8,128)} fusion(bf16[1,5376,1344]{1,2,0:T(8,128)(2,1)} %all-gather.27.cloned.1.call-done, bf16[5376,128]{1,0:T(8,128)(2,1)} %all-gather.19.cloned.1.call-done, bf16[1,1344,5376]{2,1,0:T(8,128)(2,1)} %all-gather.23.cloned.1.call-done, f32[128,1344]{0,1:T(8,128)S(1)} %fusion.8), kind=kOutput, calls=%fused_computation.21 | convolution fusion | flops 3700924416 | bytes 33718272 | tf_op jit(solution)/shard_map/dot_general | solution.py:34
  976.9 64.4 %reduce-scatter.22.cloned.1.call-done = f32[336,128]{1,0:T(8,128)} async-done(((f32[5376,128]{1,0:T(8,128)}), f32[336,128]{1,0:T(8,128)}) %reduce-scatter.22.cloned.1.call-update) | async-done | bytes 172048
  1050.0 31.4 %all-gather.21.cloned.1.call-done = bf16[5376,128]{1,0:T(8,128)(2,1)} async-done(((bf16[336,128]{1,0:T(8,128)(2,1)}), bf16[5376,128]{1,0:T(8,128)(2,1)}) %all-gather.21.cloned.1.call-update) | async-done | bytes 1376272 | tf_op jit(solution)/shard_map/all_gather | solution.py:40
  1081.4 21.4 %fusion.27 = f32[5376,128]{0,1:T(8,128)} fusion(bf16[1,5376,1344]{1,2,0:T(8,128)(2,1)} %all-gather.27.cloned.1.call-done, bf16[5376,128]{1,0:T(8,128)(2,1)} %all-gather.21.cloned.1.call-done, bf16[1,1344,5376]{2,1,0:T(8,128)(2,1)} %all-gather.23.cloned.1.call-done, f32[128,1344]{0,1:T(8,128)S(1)} %fusion.8), kind=kOutput, calls=%fused_computation.22 | convolution fusion | flops 3700924416 | bytes 33718272 | tf_op jit(solution)/shard_map/dot_general | solution.py:34
  1108.1 13.4 all-gather.3
  1128.2 53.3 %psum.51 = f32[128,64]{0,1:T(8,128)S(1)} all-reduce(f32[128,64]{0,1:T(8,128)S(1)} %fusion.75), channel_id=1, replica_groups=mesh['section'=4,'tensor'=16,'dp'=2] {'tensor'}, use_global_device_ids=true, to_apply=%region_9.10 | all-reduce | flops 8192 | bytes 65536 | tf_op jit(solution)/shard_map/psum | solution.py:104
  1187.4 91.2 %all-reduce.5.cloned.1.call-done = f32[256,64]{0,1:T(8,128)} async-done(((f32[256,64]{0,1:T(8,128)}), f32[256,64]{0,1:T(8,128)}) %all-reduce.5.cloned.1.call-update) | async-done | bytes 65552 | tf_op jit(solution)/shard_map/psum | solution.py:104
  1278.7 149.1 %all-reduce.7.cloned.1.call-done = (f32[256,64]{0,1:T(8,128)}, f32[256,64]{0,1:T(8,128)}, f32[256,64]{0,1:T(8,128)}) async-done(((f32[256,64]{0,1:T(8,128)}, f32[256,64]{0,1:T(8,128)}, f32[256,64]{0,1:T(8,128)}), (f32[256,64]{0,1:T(8,128)}, f32[256,64]{0,1:T(8,128)}, f32[256,64]{0,1:T(8,128)})) %all-reduce.7.cloned.1.call-update) | async-done | bytes 196624 | tf_op jit(solution)/shard_map/psum | solution.py:53
  (98 shorter events, 81.8 us)
Async XLA Ops:
  7.2 1174.4 %copy-start = (bf16[1,64,5376]{2,1,0:T(8,128)(2,1)S(1)}, bf16[1,64,5376]{2,1,0:T(8,128)(2,1)}, u32[]{:S(2)}) copy-start(bf16[1,64,5376]{2,1,0:T(8,128)(2,1)} %param.19) | copy-start | bytes 2064388
  7.2 44.6 %all-gather.13.cloned.1.call-start = ((), (), s32[]{:S(2)}) async-start(), calls=%async_computation.5 | async-start | bytes 2924544 | tf_op jit(solution)/shard_map/all_gather | solution.py:40
  15.5 253.3 %reduce-scatter.16.cloned.1.call-start = ((), (), s32[]{:S(2)}) async-start(), calls=%async_computation.14 | async-start | bytes 5849088
  15.6 170.4 %copy-start.9 = (s32[1024]{0:T(1024)}, s32[1024]{0:T(1024)S(1)}, u32[]{:S(2)}) copy-start(s32[1024]{0:T(1024)S(1)} %iota_add_fusion) | copy-start | bytes 12292
  15.6 170.4 %copy-start.10 = (s32[256]{0:T(256)S(1)}, s32[256]{0:T(256)}, u32[]{:S(2)}) copy-start(s32[256]{0:T(256)} %param.17) | copy-start | bytes 3076
  201.3 117.4 %all-gather.25.cloned.1.call-start = ((), (), s32[]{:S(2)}) async-start(), calls=%async_computation.12 | async-start | bytes 1462272 | tf_op jit(solution)/shard_map/all_gather | solution.py:40
  202.1 279.2 %all-gather.27.cloned.1.call-start = ((), (), s32[]{:S(2)}) async-start(), calls=%async_computation.13 | async-start | bytes 21676032 | tf_op jit(solution)/shard_map/all_gather | solution.py:83
  202.7 456.8 %all-gather.23.cloned.1.call-start = ((), (), s32[]{:S(2)}) async-start(), calls=%async_computation.11 | async-start | bytes 21676032 | tf_op jit(solution)/shard_map/all_gather | solution.py:84
  203.2 490.4 %all-gather.15.cloned.1.call-start = ((), (), s32[]{:S(2)}) async-start(), calls=%async_computation.6 | async-start | bytes 1462272 | tf_op jit(solution)/shard_map/all_gather | solution.py:40
  318.2 464.6 %reduce-scatter.18.cloned.1.call-start = ((), (), s32[]{:S(2)}) async-start(), calls=%async_computation.15 | async-start | bytes 2924544
  718.3 104.6 %all-gather.17.cloned.1.call-start = ((), (), s32[]{:S(2)}) async-start(), calls=%async_computation.7 | async-start | bytes 1462272 | tf_op jit(solution)/shard_map/all_gather | solution.py:40
  783.9 6.5 collective-permute-start
  791.2 120.9 %reduce-scatter.20.cloned.1.call-start = ((), (), s32[]{:S(2)}) async-start(), calls=%async_computation.16 | async-start | bytes 2924544
  847.6 104.6 %all-gather.19.cloned.1.call-start = ((), (), s32[]{:S(2)}) async-start(), calls=%async_computation.8 | async-start | bytes 1462272 | tf_op jit(solution)/shard_map/all_gather | solution.py:40
  913.1 6.5 collective-permute-start.1
  920.4 120.9 %reduce-scatter.22.cloned.1.call-start = ((), (), s32[]{:S(2)}) async-start(), calls=%async_computation.17 | async-start | bytes 2924544
  976.8 104.6 %all-gather.21.cloned.1.call-start = ((), (), s32[]{:S(2)}) async-start(), calls=%async_computation.9 | async-start | bytes 1462272 | tf_op jit(solution)/shard_map/all_gather | solution.py:40
  1042.4 6.5 collective-permute-start.2
  1049.7 135.1 %reduce-scatter.24.cloned.1.call-start = ((), (), s32[]{:S(2)}) async-start(), calls=%async_computation.18 | async-start | bytes 2924544
  1106.1 18.3 %copy-start.7 = (bf16[64,1024]{1,0:T(8,128)(2,1)S(1)}, bf16[64,1024]{1,0:T(8,128)(2,1)}, u32[]{:S(2)}) copy-start(bf16[64,1024]{1,0:T(8,128)(2,1)} %param.20) | copy-start | bytes 393220
  1106.1 172.5 %all-reduce.5.cloned.1.call-start = ((), (), s32[]{:S(2)}) async-start(), calls=%async_computation.10 | async-start | bytes 131072 | tf_op jit(solution)/shard_map/psum | solution.py:104
  1107.8 319.9 %all-reduce.7.cloned.1.call-start = ((), (), s32[]{:S(2)}) async-start(), calls=%async_computation.19 | async-start | bytes 393216 | tf_op jit(solution)/shard_map/psum | solution.py:53
  1121.5 60.1 %copy-start.1 = (bf16[5376,128]{1,0:T(8,128)(2,1)S(1)}, bf16[5376,128]{1,0:T(8,128)(2,1)}, u32[]{:S(2)}) copy-start(bf16[5376,128]{1,0:T(8,128)(2,1)} %all-gather.15.cloned.1.call-done) | copy-start | bytes 4128772
  1181.6 2.8 copy-start.3
  (5 other events, 6.6 us)
Sparse Core Ops, SparseCore 0:
  15.6 36.1 all-gather.12
  201.5 67.2 reduce-scatter.15
  270.6 32.0 all-gather.24
  304.3 176.9 all-gather.26
  482.9 176.4 all-gather.22
  661.1 32.4 all-gather.14
  718.4 64.3 reduce-scatter.17
  791.3 31.5 all-gather.16
  847.7 64.3 reduce-scatter.19
  920.5 31.5 all-gather.18
  976.9 64.3 reduce-scatter.21
  1049.8 31.5 all-gather.20
  1106.2 65.8 reduce-scatter.23
  1174.6 103.9 all-reduce.4
  1283.6 144.1 all-reduce.6
where the time goes:
time: 1450 us; the launch traced here: 1440 us
  waiting for transfers between devices  1010 us (70%)
  blocking collectives  249 us (17%)
  matrix products  120 us (8%)
  local copies, waits for them, and re-layouts  32.2 us (2%)
  between operations  14.5 us (1%)
    unnamed x20, waiting for transfers between devices  261 us
    all_gather x1, waiting for transfers between devices, shards(): lax.all_gather(w_down[0], 'dp', axis=0, tiled=True)  171 us
    all_gather x6, waiting for transfers between devices, feature_fold(): lax.all_gather(operand, 'tensor', axis=0, tiled=True)  165 us
    all_gather x1, waiting for transfers between devices, shards(): lax.all_gather(w_up[0], 'dp', axis=1, tiled=True)  163 us
    psum x1, waiting for transfers between devices, vocab_sums(): return lax.psum(operand, ('section', 'tensor', 'dp'))  149 us
    dot_general x16, matrix products, contract(): lax.dot_general(left, right, (((left_dim,), (right_dim,)), ((), ())), pre...  117 us
    psum x1, waiting for transfers between devices, shards(): lax.psum((contract(activated, pin_full, 1, 1), dim_term), 'tensor')  91.2 us
    pmax x1, blocking collectives, shards(): row_peak = lax.pmax(local_peak, ('section', 'tensor', 'dp'))  64.3 us
  transfers between devices with their start and end apart: 18, of which 16 were waited for; matrix products, arithmetic and copies ran while one was open for 2% of the time, Pallas kernels for 0%

commit v1 on v0

v1 whole, which is shorter than its diff:
```python
import math

import jax
import jax.numpy as jnp
from jax import lax
from jax.experimental import pallas as pl
from jax.experimental.pallas import tpu as pltpu
from jax.sharding import PartitionSpec as P

D = 5376
TOK = 256
SEQ = 128
RANK = 64
UNITS = 672
VROWS = 1024
ROWS = 336
KB = 768
NB = D // KB
PAD = 768
BF = jnp.bfloat16
F32 = jnp.float32


def dot(a, b, dims=((1,), (0,)), precision=None):
    return lax.dot_general(a, b, (dims, ((), ())), preferred_element_type=F32, precision=precision)


def outer_pair(left, right):
    parts = [
        dot(left[:, q * SEQ:(q + 1) * SEQ], right[:, q * SEQ:(q + 1) * SEQ], ((1,), (1,)), lax.Precision.HIGHEST)
        for q in range(2)
    ]
    return jnp.concatenate(parts, axis=1)


def kernel(
    x_hbm, fh_hbm, wup_hbm, wdn_hbm, tab_hbm, tok, tgt, pin, pout, pvoc, pdim,
    lay_out, tab_out,
    tab, wup, wdn, fh, xb, cot,
    ph, pc, r0, r1, r2, s1, q0, q1, q2, u1, zr,
    logits, gradt, hid, slope, hgrad, inproj, vside, own,
    sm_cur, sm_slot, st_cur, st_slot, la_cur, la_slot, ta_cur, ta_slot,
    lsem, ag_send, ag_recv, rs_send, rs_recv, z_send, z_recv, c_send, c_recv, ar_send, ar_recv,
):
    sec = lax.axis_index("section")
    ten = lax.axis_index("tensor")
    dp = lax.axis_index("dp")
    c = ten % 2
    y = (ten // 2) % 4
    x = dp * 2 + ten // 8

    def dev(xx, yy, cc, zz):
        return (zz, (xx % 2) * 8 + yy * 2 + cc, xx // 2)

    def at(ka, kb):
        return (x + ka * (1 - c) + kb * c) % 4, (y + ka * c + kb * (1 - c)) % 4

    def cidx(xx, yy, cc):
        return xx * 8 + yy * 2 + cc

    def piece(ref, i):
        return ref.at[pl.ds(pl.multiple_of(i * ROWS, 16), ROWS)]

    def rows(i):
        return pl.ds(pl.multiple_of(i * ROWS, 16), ROWS)

    def rc(src, dst, ssem, rsem, device):
        return pltpu.make_async_remote_copy(
            src_ref=src, dst_ref=dst, send_sem=ssem, recv_sem=rsem,
            device_id=device, device_id_type=pl.DeviceIdType.MESH,
        )

    sib = dev(x, y, 1 - c, sec)
    mine = cidx(x, y, c)

    local = [
        pltpu.make_async_copy(fh_hbm, piece(fh, mine), lsem.at[0]),
        pltpu.make_async_copy(x_hbm, piece(xb, mine), lsem.at[1]),
        pltpu.make_async_copy(tab_hbm, tab, lsem.at[2]),
        pltpu.make_async_copy(wup_hbm, wup, lsem.at[3]),
        pltpu.make_async_copy(wdn_hbm, wdn, lsem.at[4]),
    ]
    for copy in local:
        copy.start()

    barrier = pltpu.get_barrier_semaphore()
    partners = [sib]
    for k in range(1, 4):
        partners.append(dev((x + k) % 4, y, c, sec))
        partners.append(dev(x, (y + k) % 4, c, sec))
        partners.append(dev(x, y, c, (sec + k) % 4))
    for partner in partners:
        pl.semaphore_signal(barrier, inc=1, device_id=partner, device_id_type=pl.DeviceIdType.MESH)
    pl.semaphore_wait(barrier, len(partners))

    def ag_copy(n, buf, i, device):
        return rc(piece(buf, i), piece(buf, i), ag_send.at[n], ag_recv.at[n, i], device)

    def ag_first(n, buf):
        for k in range(1, 4):
            xx, yy = at(k, 0)
            ag_copy(n, buf, mine, dev(xx, yy, c, sec)).start()
        ag_copy(n, buf, mine, sib).start()

    def ag_second(n, buf):
        for ka in range(4):
            xx, yy = at(4 - ka, 0)
            i = cidx(xx, yy, c)
            if ka:
                ag_copy(n, buf, i, sib).wait_recv()
            for kb in range(1, 4):
                xx, yy = at(0, kb)
                ag_copy(n, buf, i, dev(xx, yy, c, sec)).start()
            if ka:
                ag_copy(n, buf, i, sib).start()

    def ag_third(n, buf):
        def body(j, carry):
            xx, yy = at(4 - j % 4, 3 - j // 4)
            i = cidx(xx, yy, c)
            ag_copy(n, buf, i, sib).wait_recv()
            ag_copy(n, buf, i, sib).start()
            return carry

        lax.fori_loop(0, 12, body, 0)

    def ag_last(n, buf):
        def body(j, carry):
            ag_copy(n, buf, cidx(j // 4, j % 4, 1 - c), sib).wait_recv()
            return carry

        lax.fori_loop(0, 16, body, 0)

    def ag_drain(n, buf):
        part = buf.at[pl.ds(0, 31 * ROWS)]
        rc(part, part, ag_send.at[n], ag_recv.at[n, 0], sib).wait_send()

    def rs(n, src, pair, store, b0, b1, b2, held):
        def to_sibling(j, carry):
            t = 2 * j + 1 - c
            if store:
                for r, value in enumerate(pair(t)):
                    src[rows(r * 16 + t), :] = value.astype(BF)
            for r in range(2):
                slot = r * 8 + j
                rc(piece(src, r * 16 + t), piece(b0, slot), rs_send.at[n], rs_recv.at[n, slot], sib).start()
            return carry

        lax.fori_loop(0, 8, to_sibling, 0)
        first = x * (1 - c) + y * c

        def to_first(j, carry):
            t = 2 * j + c
            values = pair(t)
            for r in range(2):
                slot = r * 8 + j
                xx = r * 2 + j // 4
                yy = j % 4
                rc(piece(b0, slot), piece(b0, slot), rs_send.at[n], rs_recv.at[n, slot], sib).wait_recv()
                src[rows(r * 16 + t), :] = (values[r] + b0[rows(slot), :].astype(F32)).astype(BF)
                aa = xx * (1 - c) + yy * c
                bb = yy * (1 - c) + xx * c
                k = (aa - first + 4) % 4

                @pl.when(k != 0)
                def _():
                    px, py = at(k, 0)
                    spot = (k - 1) * 4 + bb
                    rc(
                        piece(src, r * 16 + t), piece(b1, spot), rs_send.at[n], rs_recv.at[n, 16 + spot],
                        dev(px, py, c, sec),
                    ).start()

            return carry

        lax.fori_loop(0, 8, to_first, 0)
        second = y * (1 - c) + x * c
        for kb in (1, 2, 3, 0):
            xx, yy = at(0, kb)
            bb = (second + kb) % 4
            total = src[rows(cidx(xx, yy, c)), :].astype(F32)
            for k in range(3):
                spot = k * 4 + bb
                rc(piece(b1, spot), piece(b1, spot), rs_send.at[n], rs_recv.at[n, 16 + spot], sib).wait_recv()
                total = total + b1[rows(spot), :].astype(F32)
            if kb:
                held[rows(kb - 1), :] = total.astype(BF)
                rc(
                    piece(held, kb - 1), piece(b2, kb - 1), rs_send.at[n], rs_recv.at[n, 27 + kb],
                    dev(xx, yy, c, sec),
                ).start()
        for k in range(3):
            rc(piece(b2, k), piece(b2, k), rs_send.at[n], rs_recv.at[n, 28 + k], sib).wait_recv()
            total = total + b2[rows(k), :].astype(F32)
        return total

    def rs_drain(n, src):
        part = src.at[pl.ds(0, 31 * ROWS)]
        rc(part, part, rs_send.at[n], rs_recv.at[n, 0], sib).wait_send()

    def ar_peers(phase):
        if phase == 0:
            return [(0, sib)]
        if phase == 1:
            return [(k, dev((x + k) % 4, y, c, sec)) for k in (1, 2, 3)]
        if phase == 2:
            return [(3 + k, dev(x, (y + k) % 4, c, sec)) for k in (1, 2, 3)]
        return [(6 + k, dev(x, y, c, (sec + k) % 4)) for k in (1, 2, 3)]

    def ar_copies(n, cur, slot, phase):
        return [
            rc(cur.at[phase], slot.at[s], ar_send.at[n], ar_recv.at[n, s], device)
            for s, device in ar_peers(phase)
        ]

    def ar_start(n, cur, slot, phase):
        for copy in ar_copies(n, cur, slot, phase):
            copy.start()

    def ar_wait(n, cur, slot, phase):
        for copy in ar_copies(n, cur, slot, phase):
            copy.wait_recv()

    def ar_sum(n, cur, slot, phase):
        ar_wait(n, cur, slot, phase)
        total = cur[phase].astype(F32)
        for s, _ in ar_peers(phase):
            total = total + slot[s].astype(F32)
        cur[phase + 1] = total.astype(cur.dtype)

    def ar_drain(n, slot, count):
        part = slot.at[pl.ds(0, count)]
        rc(part, part, ar_send.at[n], ar_recv.at[n, 0], sib).wait_send()

    local[0].wait()
    ag_first(0, fh)
    local[1].wait()

    columns = ((sec * 16 + ten) * 2 + dp) * VROWS + lax.broadcasted_iota(jnp.int32, (VROWS, TOK), 0)
    dim_part = dot(pdim[...], fh[rows(mine), :])
    dim_part = jnp.where(sec == 0, dim_part, jnp.zeros_like(dim_part))
    blank = jnp.zeros_like(dim_part)
    sm_cur[0, 0:RANK, 0:SEQ] = jnp.where(dp == 0, dim_part, blank).astype(BF)
    sm_cur[0, 0:RANK, SEQ:TOK] = jnp.where(dp == 1, dim_part, blank).astype(BF)
    token_hot = jnp.where(tok[...] == columns, 1.0, 0.0).astype(BF)
    sm_cur[0, RANK:2 * RANK, :] = dot(pvoc[...], token_hot).astype(BF)

    ag_second(0, fh)
    ar_start(0, sm_cur, sm_slot, 0)
    ag_third(0, fh)
    ag_first(1, xb)
    ag_last(0, fh)

    local[2].wait()
    logits[...] = jnp.zeros_like(logits)

    def logit_step(b, carry):
        k0 = pl.multiple_of(b * KB, KB)
        k1 = pl.multiple_of(D + b * KB, KB)
        right = jnp.concatenate([fh[pl.ds(k0, KB), :], fh[pl.ds(k1, KB), :]], axis=1)
        logits[...] += dot(tab[:, pl.ds(k0, KB)], right)
        return carry

    lax.fori_loop(0, NB, logit_step, 0)
    ag_second(1, xb)
    ar_sum(0, sm_cur, sm_slot, 0)
    ar_start(0, sm_cur, sm_slot, 1)

    peak = jnp.max(logits[...], axis=0, keepdims=True)
    st_cur[0] = jnp.zeros((8, TOK), F32)
    st_cur[0, 0:1, :] = peak
    st_cur[0, 1:2, :] = jnp.sum(jnp.exp(logits[...] - peak), axis=0, keepdims=True)
    ar_start(1, st_cur, st_slot, 0)
    ag_third(1, xb)

    def stats_step(phase):
        ar_wait(1, st_cur, st_slot, phase)
        peaks = [st_cur[phase, 0:1, :]] + [st_slot[s, 0:1, :] for s, _ in ar_peers(phase)]
        sums = [st_cur[phase, 1:2, :]] + [st_slot[s, 1:2, :] for s, _ in ar_peers(phase)]
        top = peaks[0]
        for other in peaks[1:]:
            top = jnp.maximum(top, other)
        total = jnp.zeros_like(top)
        for a, b in zip(peaks, sums):
            total = total + b * jnp.exp(a - top)
        st_cur[phase + 1] = jnp.zeros((8, TOK), F32)
        st_cur[phase + 1, 0:1, :] = top
        st_cur[phase + 1, 1:2, :] = total
        if phase < 3:
            ar_start(1, st_cur, st_slot, phase + 1)

    stats_step(0)
    local[3].wait()
    ag_last(1, xb)
    stats_step(1)

    hid[...] = jnp.zeros_like(hid)

    def hidden_step(b, carry):
        k0 = pl.multiple_of(b * KB, KB)
        k1 = pl.multiple_of(D + b * KB, KB)
        left = jnp.concatenate([xb[pl.ds(k0, KB), :], xb[pl.ds(k1, KB), :]], axis=1)
        hid[:, 0:UNITS] += dot(left.T, wup[pl.ds(k0, KB), :])
        return carry

    lax.fori_loop(0, 4, hidden_step, 0)
    stats_step(2)
    lax.fori_loop(4, NB, hidden_step, 0)
    stats_step(3)

    top = st_cur[4, 0:1, :]
    scale = 1.0 / st_cur[4, 1:2, :]
    hot = jnp.where(tgt[...] == columns, 1.0, 0.0)
    grad = jnp.exp(logits[...] - top) * scale - hot
    logits[...] = grad
    gradt[...] = grad.T.astype(BF)

    def head_step(b, carry):
        k0 = pl.multiple_of(b * KB, KB)
        k1 = pl.multiple_of(D + b * KB, KB)
        block = dot(gradt[...], tab[:, pl.ds(k0, KB)]).T.astype(BF)
        ph[pl.ds(k0, KB), :] = block[:, 0:SEQ]
        ph[pl.ds(k1, KB), :] = block[:, SEQ:TOK]
        return carry

    lax.fori_loop(0, NB, head_step, 0)

    def head_pair(t):
        return ph[rows(t), :].astype(F32), ph[rows(16 + t), :].astype(F32)

    ar_sum(0, sm_cur, sm_slot, 1)
    ar_start(0, sm_cur, sm_slot, 2)
    own[...] = rs(0, ph, head_pair, False, r0, r1, r2, s1)

    @pl.when(sec != 3)
    def _():
        zr[rows(3), :] = own[...].astype(BF)
        rc(piece(zr, 3), piece(zr, sec), z_send, z_recv.at[sec], dev(x, y, c, 3)).start()

    hidden = hid[...].T[0:UNITS, :]
    gate = jax.nn.sigmoid(hidden)
    slope[...] = gate * (1.0 + hidden * (1.0 - gate))
    inproj[...] = dot(pin[...], (hidden * gate).astype(BF))
    vside[...] = dot(pvoc[...], logits[...].astype(BF))
    local[4].wait()

    ar_sum(0, sm_cur, sm_slot, 2)
    ar_start(0, sm_cur, sm_slot, 3)

    @pl.when(sec == 3)
    def _():
        total = own[...]
        for s in range(3):
            rc(piece(zr, s), piece(zr, s), z_send, z_recv.at[s], sib).wait_recv()
            total = total + zr[rows(s), :].astype(F32)
        cot[rows(mine), :] = total.astype(BF)

    @pl.when(sec != 3)
    def _():
        rc(piece(cot, mine), piece(cot, mine), c_send, c_recv, sib).wait_recv()

    ag_first(2, cot)
    ag_second(2, cot)
    ag_third(2, cot)
    ag_last(2, cot)
    hid_rows = hgrad
    act = jnp.zeros((UNITS, TOK), F32)

    def down_step(b, acc):
        k0 = pl.multiple_of(b * KB, KB)
        k1 = pl.multiple_of(D + b * KB, KB)
        right = jnp.concatenate([cot[pl.ds(k0, KB), :], cot[pl.ds(k1, KB), :]], axis=1)
        return acc + dot(wdn[:, pl.ds(k0, KB)], right)

    act = lax.fori_loop(0, NB, down_step, act)
    hid_rows[...] = (act * slope[...]).astype(BF)

    def back_pair(t):
        block = dot(wup[rows(t), :], hgrad[...])
        return block[:, 0:SEQ], block[:, SEQ:TOK]

    back = rs(1, pc, back_pair, True, q0, q1, q2, u1)
    own[...] = (back + cot[rows(mine), :].astype(F32)).astype(BF).astype(F32)

    @pl.when(sec != 0)
    def _():
        zr[rows(4), :] = own[...].astype(BF)
        rc(piece(zr, 4), piece(cot, mine), c_send, c_recv, dev(x, y, c, (sec + 3) % 4)).start()

    def out_step(b, acc):
        k0 = pl.multiple_of(b * KB, KB)
        k1 = pl.multiple_of(D + b * KB, KB)
        right = jnp.concatenate([cot[pl.ds(k0, KB), :], cot[pl.ds(k1, KB), :]], axis=1)
        return acc + dot(pout[:, pl.ds(k0, KB)], right)

    outproj = lax.fori_loop(0, NB, out_step, jnp.zeros((RANK, TOK), F32))
    la_cur[0] = outer_pair(outproj, inproj[...])
    ar_start(2, la_cur, la_slot, 0)
    ar_sum(0, sm_cur, sm_slot, 3)
    ta_cur[0] = outer_pair(vside[...], sm_cur[4, 0:RANK, :].astype(F32))

    @pl.when(sec == 0)
    def _():
        embed = math.sqrt(D) * dot(pdim[...], own[...].astype(BF))
        first = jnp.where(dp == 0, embed, jnp.zeros_like(embed))
        second = jnp.where(dp == 1, embed, jnp.zeros_like(embed))
        both = jnp.concatenate([first, second], axis=1)
        ta_cur[0] += outer_pair(sm_cur[4, RANK:2 * RANK, :].astype(F32), both)

    ar_start(3, ta_cur, ta_slot, 0)
    for phase in range(3):
        ar_sum(2, la_cur, la_slot, phase)
        if phase < 2:
            ar_start(2, la_cur, la_slot, phase + 1)
        ar_sum(3, ta_cur, ta_slot, phase)
        ar_start(3, ta_cur, ta_slot, phase + 1)
    lay_out[...] = jnp.where(dp == 0, la_cur[3, :, 0:RANK], la_cur[3, :, RANK:2 * RANK])
    ar_sum(3, ta_cur, ta_slot, 3)
    tab_out[...] = jnp.where(dp == 0, ta_cur[4, :, 0:RANK], ta_cur[4, :, RANK:2 * RANK])

    ag_drain(0, fh)
    ag_drain(1, xb)
    ag_drain(2, cot)
    rs_drain(0, ph)
    rs_drain(1, pc)
    ar_drain(0, sm_slot, 10)
    ar_drain(1, st_slot, 10)
    ar_drain(2, la_slot, 7)
    ar_drain(3, ta_slot, 10)

    @pl.when(sec != 3)
    def _():
        rc(piece(zr, 3), piece(zr, 3), z_send, z_recv.at[0], sib).wait_send()

    @pl.when(sec != 0)
    def _():
        rc(piece(zr, 4), piece(zr, 4), c_send, c_recv, sib).wait_send()


def shards(x_in, final_hidden, w_up, w_down, table, token_ids, targets, proj_in, proj_out, proj_vocab, proj_dim):
    vmem = pl.BlockSpec(memory_space=pltpu.VMEM)
    hbm = pl.BlockSpec(memory_space=pl.ANY)
    full = lambda n: pltpu.VMEM((n * ROWS, SEQ), BF)
    dma = pltpu.SemaphoreType.DMA
    layer, tab = pl.pallas_call(
        kernel,
        out_shape=[jax.ShapeDtypeStruct((RANK, RANK), F32)] * 2,
        in_specs=[hbm] * 5 + [vmem] * 6,
        out_specs=[vmem] * 2,
        scratch_shapes=[
            pltpu.VMEM((VROWS, D), BF),
            pltpu.VMEM((D, UNITS), BF),
            pltpu.VMEM((UNITS, D), BF),
            full(32), full(32), full(32),
            full(32), full(32),
            full(16), full(12), full(3), full(3),
            full(16), full(12), full(3), full(3),
            full(5),
            pltpu.VMEM((VROWS, TOK), F32),
            pltpu.VMEM((TOK, VROWS), BF),
            pltpu.VMEM((TOK, PAD), F32),
            pltpu.VMEM((UNITS, TOK), F32),
            pltpu.VMEM((UNITS, TOK), BF),
            pltpu.VMEM((RANK, TOK), F32),
            pltpu.VMEM((RANK, TOK), F32),
            pltpu.VMEM((ROWS, SEQ), F32),
            pltpu.VMEM((5, 2 * RANK, TOK), BF),
            pltpu.VMEM((10, 2 * RANK, TOK), BF),
            pltpu.VMEM((5, 8, TOK), F32),
            pltpu.VMEM((10, 8, TOK), F32),
            pltpu.VMEM((5, RANK, 2 * RANK), F32),
            pltpu.VMEM((10, RANK, 2 * RANK), F32),
            pltpu.VMEM((5, RANK, 2 * RANK), F32),
            pltpu.VMEM((10, RANK, 2 * RANK), F32),
            dma((5,)),
            dma((3,)), dma((3, 32)),
            dma((2,)), dma((2, 31)),
            dma(()), dma((3,)),
            dma(()), dma(()),
            dma((4,)), dma((4, 10)),
        ],
        compiler_params=pltpu.CompilerParams(
            collective_id=0, has_side_effects=True, vmem_limit_bytes=62 * 1024 * 1024
        ),
    )(
        x_in[0], final_hidden, w_up[0], w_down[0], table,
        token_ids.reshape(1, TOK), targets.reshape(1, TOK),
        proj_in[0], proj_out[0], proj_vocab, proj_dim,
    )
    return layer[None, None], tab[None]


def solution(mesh):
    placed = (
        P("section", "tensor", "dp"),
        P("tensor", "dp"),
        P("section", None, ("tensor", "dp")),
        P("section", ("tensor", "dp"), None),
        P(("section", "tensor", "dp"), None),
        P(),
        P(),
        P("section", None, ("tensor", "dp")),
        P("section", None, None),
        P(None, ("section", "tensor", "dp")),
        P(None, "tensor"),
    )
    return jax.shard_map(
        shards,
        mesh=mesh,
        in_specs=placed,
        out_specs=(P("section", "dp", None, None), P("dp", None, None)),
        check_vma=False,
    )
```

time: 1450 us -> 276 us (0.19)
  waiting for transfers between devices: 1010 us -> 0 us
  Pallas kernels: 0 us -> 261 us
  blocking collectives: 249 us -> 0 us
  matrix products: 120 us -> 0 us
  local copies, waits for them, and re-layouts: 32.2 us -> 14.1 us
    all_gather x8 -> x0, waiting for transfers between devices: 498 us -> none  [the longest x1 171 us: shards(): lax.all_gather(w_down[0], 'dp', axis=0, tiled=True)]
    pallas_call x0 -> x1, Pallas kernels: none -> 261 us  [shards(): pl.pallas_call(kernel, out_shape=[jax.ShapeDtypeStruct((RANK, RANK), F32)...]
    unnamed x20 -> x0, waiting for transfers between devices: 261 us -> none
    psum x2 -> x0, waiting for transfers between devices: 240 us -> none  [the longest x1 149 us: vocab_sums(): return lax.psum(operand, ('section', 'tensor', 'dp'))]
    psum x3 -> x0, blocking collectives: 163 us -> none  [the longest x1 62.7 us: vocab_sums(): return lax.psum(operand, ('section', 'tensor', 'dp'))]
    dot_general x19 -> x0, matrix products: 120 us -> none  [the longest x16 117 us: contract(): lax.dot_general(left, right, (((left_dim,), (right_dim,)), ((), ())), pre...]
    pmax x1 -> x0, blocking collectives: 64.3 us -> none  [shards(): row_peak = lax.pmax(local_peak, ('section', 'tensor', 'dp'))]
    all_gather x2 -> x0, blocking collectives: 21.6 us -> none  [the longest x1 13.4 us: shards(): lax.all_gather(proj_in[0], 'dp', axis=1, tiled=True)]
  transfers between devices with their start and end apart: 18 -> 0, of which waited for: 16 -> 0; matrix products, arithmetic and copies ran while one was open for 2% -> 0% of each run, Pallas kernels for 0% -> 0%
where the time goes in v1:
time: 276 us
  Pallas kernels  261 us (95%)
  local copies, waits for them, and re-layouts  14.1 us (5%)
    pallas_call x1, Pallas kernels, shards(): pl.pallas_call(kernel, out_shape=[jax.ShapeDtypeStruct((RANK, RANK), F32)...  261 us
    unnamed x3, local copies, waits for them, and re-layouts  14.1 us

profile of v1, /device:TPU:32, one launch (start us, length us, event | category | flops | bytes accessed | tf_op | source)
XLA Modules:
  0.0 275.8 jit_solution(6838675062724350127)
XLA Ops:
  0.6 11.4 %copy.13 = bf16[1,5376,672]{2,1,0:T(8,128)(2,1)} copy(bf16[1,5376,672]{1,2,0:T(8,128)(2,1)} %param.13) | data formatting | bytes 14450688 | tf_op args[2]
  12.0 261.1 %shard_map.122 = (f32[64,64]{1,0:T(8,128)}, f32[64,64]{1,0:T(8,128)}) custom-call(bf16[336,128]{1,0:T(8,128)(2,1)} %bitcast.13, bf16[336,128]{1,0:T(8,128)(2,1)} %fh_hbm.1, bf16[5376,672]{1,0:T(8,128)(2,1)} %bitcast.9, bf16[672,5376]{1,0:T(8,128)(2,1)} %bitcast.10, bf16[1024,5376]{1,0:T(8,128)(2,1)} %tab_hbm.1, s32[1,256]{1,0:T(1,128)} %bitcast.16, ...), custom_call_target="tpu_custom_call" | custom-call | tf_op jit(solution)/shard_map/pallas_call | solution.py:445
  273.1 1.4 copy.16
  274.5 1.4 copy.17

commit v2 on v1

v2 whole, which is shorter than its diff:
```python
import math

import jax
import jax.numpy as jnp
from jax import lax
from jax.experimental import pallas as pl
from jax.experimental.pallas import tpu as pltpu
from jax.sharding import PartitionSpec as P

D = 5376
TOK = 256
SEQ = 128
RANK = 64
UNITS = 672
VROWS = 1024
ROWS = 336
PARTS = 3
SUB = ROWS // PARTS
PART = D // PARTS
HALF = D // 2
TB = 384
HB = 896
BF = jnp.bfloat16
F32 = jnp.float32


def dot(a, b, dims=((1,), (0,)), precision=None):
    return lax.dot_general(a, b, (dims, ((), ())), preferred_element_type=F32, precision=precision)


def outer_pair(left, right):
    parts = [
        dot(left[:, q * SEQ:(q + 1) * SEQ], right[:, q * SEQ:(q + 1) * SEQ], ((1,), (1,)), lax.Precision.HIGHEST)
        for q in range(2)
    ]
    return jnp.concatenate(parts, axis=1)


def kernel(
    x_hbm, fh_hbm, wupt_hbm, wdn_hbm, tab_hbm, tok, tgt, pin, pout, pvoc, pdim,
    lay_out, tab_out,
    tab, wupt, wup, wdn, fh, xb, cot, pdt,
    r0, r1, r2, zr,
    logits, gradt, act, slope, hgrad, inproj, vside, upside, own, sums,
    sm_cur, sm_slot, st_cur, st_slot, la_cur, la_slot, ta_cur, ta_slot,
    lsem, ag_send, ag_recv, rs_send, rs_recv, z_send, z_recv, c_send, c_recv, ar_send, ar_recv,
):
    sec = lax.axis_index("section")
    ten = lax.axis_index("tensor")
    dp = lax.axis_index("dp")
    c = ten % 2
    y = (ten // 2) % 4
    lo = ten // 8
    x = dp * 2 + lo

    def dev(xx, yy, cc, zz):
        return (zz, (xx % 2) * 8 + yy * 2 + cc, xx // 2)

    def at(ka, kb):
        return (x + ka * (1 - c) + kb * c) % 4, (y + ka * c + kb * (1 - c)) % 4

    def cidx(xx, yy, cc):
        return xx * 8 + yy * 2 + cc

    def rows(i):
        return pl.ds(pl.multiple_of(i * ROWS, 16), ROWS)

    def piece(ref, i):
        return ref.at[rows(i)]

    def span(start, count):
        return pl.ds(pl.multiple_of(start, 16), count)

    def given(xx, yy, cc, s):
        return span((xx * 8 + yy * 2 + cc) * ROWS + s * SUB, SUB)

    def chain_start(xx, yy, cc, s):
        spot = (1 - cc) * ((xx % 2) * 4 + yy) + cc * (yy * 2 + xx % 2)
        return (xx // 2) * D + s * PART + (cc * 8 + spot) * SUB

    def chained(xx, yy, cc, s):
        return span(chain_start(xx, yy, cc, s), SUB)

    def rc(src, dst, ssem, rsem, device):
        return pltpu.make_async_remote_copy(
            src_ref=src, dst_ref=dst, send_sem=ssem, recv_sem=rsem,
            device_id=device, device_id_type=pl.DeviceIdType.MESH,
        )

    sib = dev(x, y, 1 - c, sec)
    mine = cidx(x, y, c)

    local = [
        pltpu.make_async_copy(fh_hbm, piece(fh, mine), lsem.at[0]),
        pltpu.make_async_copy(x_hbm, piece(xb, mine), lsem.at[1]),
        pltpu.make_async_copy(wupt_hbm, wupt, lsem.at[2]),
        pltpu.make_async_copy(tab_hbm, tab, lsem.at[3]),
        pltpu.make_async_copy(wdn_hbm, wdn, lsem.at[4]),
    ]
    for copy in local:
        copy.start()

    barrier = pltpu.get_barrier_semaphore()
    partners = [sib]
    for k in range(1, 4):
        partners.append(dev((x + k) % 4, y, c, sec))
        partners.append(dev(x, (y + k) % 4, c, sec))
        partners.append(dev(x, y, c, (sec + k) % 4))
    for partner in partners:
        pl.semaphore_signal(barrier, inc=1, device_id=partner, device_id_type=pl.DeviceIdType.MESH)
    pl.semaphore_wait(barrier, len(partners))

    def ag_copy(n, buf, where, chip, cc, s, device):
        xx, yy = chip
        ref = buf.at[where(xx, yy, cc, s)]
        return rc(ref, ref, ag_send.at[n], ag_recv.at[n, s, cidx(xx, yy, cc)], device)

    def ag_first(n, buf, where, s):
        for k in range(1, 4):
            ag_copy(n, buf, where, (x, y), c, s, dev(*at(k, 0), c, sec)).start()
        for k in range(1, 4):
            ag_copy(n, buf, where, (x, y), c, s, dev(*at(0, k), c, sec)).start()
        ag_copy(n, buf, where, (x, y), c, s, sib).start()

    def ag_second(n, buf, where, s):
        for ka in range(1, 4):
            chip = at(4 - ka, 0)
            ag_copy(n, buf, where, chip, c, s, sib).wait_recv()
            for kb in range(1, 4):
                ag_copy(n, buf, where, chip, c, s, dev(*at(0, kb), c, sec)).start()
            ag_copy(n, buf, where, chip, c, s, sib).start()

    def ag_third(n, buf, where, s):
        def body(j, carry):
            chip = at(4 - j // 3, 3 - j % 3)
            ag_copy(n, buf, where, chip, c, s, sib).wait_recv()
            ag_copy(n, buf, where, chip, c, s, sib).start()
            return carry

        lax.fori_loop(0, 12, body, 0)

    def ag_last(n, buf, where, s):
        def body(j, carry):
            ag_copy(n, buf, where, (j // 4, j % 4), 1 - c, s, sib).wait_recv()
            return carry

        lax.fori_loop(0, 16, body, 0)

    def ag_drain(n, buf):
        whole = buf.at[pl.ds(0, 31 * ROWS)]
        rc(whole, whole, ag_send.at[n], ag_recv.at[n, 0, 0], sib).wait_send()

    b_own = y * (1 - c) + x * c

    def rs_copy(n, src, ref, start, count, sem, device, src_start):
        return rc(
            src.at[span(src_start, count)], ref.at[span(start, count)], rs_send.at[n], rs_recv.at[n, sem], device
        )

    def rs_sibling(n, src, s):
        for r in range(2):
            start = ((n * PARTS + s) * 2 + r) * 8 * SUB
            rs_copy(n, src, r0, start, 8 * SUB, s * 11 + r, sib, r * D + s * PART + (1 - c) * 8 * SUB).start()

    def pair_start(ka, u, s):
        aa = (x * (1 - c) + y * c + ka) % 4
        return chain_start(aa * (1 - c) + 2 * u * c, aa * c + 2 * u * (1 - c), c, s)

    def rs_first(n, src, s):
        for r in range(2):
            start = ((n * PARTS + s) * 2 + r) * 8 * SUB
            rs_copy(n, r0, r0, start, 8 * SUB, s * 11 + r, sib, start).wait_recv()
            here = span(r * D + s * PART + c * 8 * SUB, 8 * SUB)
            src[here, :] = (src[here, :].astype(F32) + r0[span(start, 8 * SUB), :].astype(F32)).astype(BF)
        for ka in (2, 1, 3):
            for u in range(2):
                start = ((n * PARTS + s) * 3 + ka - 1) * 4 * SUB + u * 2 * SUB
                rs_copy(
                    n, src, r1, start, 2 * SUB, s * 11 + 2 + (ka - 1) * 2 + u, dev(*at(ka, 0), c, sec),
                    pair_start(ka, u, s),
                ).start()

    def rs_second(n, src, s):
        for u in range(2):
            here = span(pair_start(0, u, s), 2 * SUB)
            total = src[here, :].astype(F32)
            for k in range(3):
                start = ((n * PARTS + s) * 3 + k) * 4 * SUB + u * 2 * SUB
                rs_copy(n, r1, r1, start, 2 * SUB, s * 11 + 2 + k * 2 + u, sib, start).wait_recv()
                total = total + r1[span(start, 2 * SUB), :].astype(F32)
            sums[pl.ds((s * 4 + u * 2) * SUB, 2 * SUB), :] = total
            src[here, :] = total.astype(BF)
        for kb in range(1, 4):
            xx, yy = at(0, kb)
            start = ((n * PARTS + s) * 3 + kb - 1) * SUB
            rs_copy(
                n, src, r2, start, SUB, s * 11 + 7 + kb, dev(xx, yy, c, sec), chain_start(xx, yy, c, s)
            ).start()

    def rs_third(n, s):
        total = sums[span((s * 4 + b_own) * SUB, SUB), :]
        for k in range(3):
            start = ((n * PARTS + s) * 3 + k) * SUB
            rs_copy(n, r2, r2, start, SUB, s * 11 + 8 + k, sib, start).wait_recv()
            total = total + r2[span(start, SUB), :].astype(F32)
        return total

    def rs_drain(n, src):
        whole = src.at[pl.ds(0, 31 * ROWS)]
        rc(whole, whole, rs_send.at[n], rs_recv.at[n, 0], sib).wait_send()

    def ar_peers(phase):
        if phase == 0:
            return [(0, sib)]
        if phase == 1:
            return [(k, dev((x + k) % 4, y, c, sec)) for k in (1, 2, 3)]
        if phase == 2:
            return [(3 + k, dev(x, (y + k) % 4, c, sec)) for k in (1, 2, 3)]
        return [(6 + k, dev(x, y, c, (sec + k) % 4)) for k in (1, 2, 3)]

    def ar_copies(n, cur, slot, phase):
        return [
            rc(cur.at[phase], slot.at[s], ar_send.at[n], ar_recv.at[n, s], device)
            for s, device in ar_peers(phase)
        ]

    def ar_start(n, cur, slot, phase):
        for copy in ar_copies(n, cur, slot, phase):
            copy.start()

    def ar_wait(n, cur, slot, phase):
        for copy in ar_copies(n, cur, slot, phase):
            copy.wait_recv()

    def ar_sum(n, cur, slot, phase):
        ar_wait(n, cur, slot, phase)
        total = cur[phase].astype(F32)
        for s, _ in ar_peers(phase):
            total = total + slot[s].astype(F32)
        cur[phase + 1] = total.astype(cur.dtype)

    def ar_drain(n, slot, count):
        part = slot.at[pl.ds(0, count)]
        rc(part, part, ar_send.at[n], ar_recv.at[n, 0], sib).wait_send()

    def feature_half(buf, h):
        return jnp.concatenate([buf[pl.ds(h * HALF, HALF), :], buf[pl.ds(D + h * HALF, HALF), :]], axis=1)

    local[0].wait()
    for s in range(PARTS):
        ag_first(0, fh, given, s)
    local[1].wait()

    columns = ((sec * 16 + ten) * 2 + dp) * VROWS + lax.broadcasted_iota(jnp.int32, (VROWS, TOK), 0)
    dim_part = dot(pdim[...], fh[rows(mine), :])
    dim_part = jnp.where(sec == 0, dim_part, jnp.zeros_like(dim_part))
    blank = jnp.zeros_like(dim_part)
    sm_cur[0, 0:RANK, 0:SEQ] = jnp.where(dp == 0, dim_part, blank).astype(BF)
    sm_cur[0, 0:RANK, SEQ:TOK] = jnp.where(dp == 1, dim_part, blank).astype(BF)
    token_hot = jnp.where(tok[...] == columns, 1.0, 0.0).astype(BF)
    sm_cur[0, RANK:2 * RANK, :] = dot(pvoc[...], token_hot).astype(BF)

    pdt[rows(mine), :] = jnp.concatenate([pdim[...].T, jnp.zeros((ROWS, SEQ - RANK), BF)], axis=1)

    for s in range(PARTS):
        ag_second(0, fh, given, s)
    ar_start(0, sm_cur, sm_slot, 0)
    local[2].wait()

    def turn(b, carry):
        k0 = pl.multiple_of(b * TB, TB)
        wup[pl.ds(k0, TB), :] = wupt[:, pl.ds(k0, TB)].T
        return carry

    lax.fori_loop(0, D // TB, turn, 0)
    for s in range(PARTS):
        ag_third(0, fh, given, s)
    for s in range(PARTS):
        ag_first(1, xb, given, s)
    for s in range(PARTS):
        ag_last(0, fh, given, s)

    local[3].wait()
    logits[...] = dot(tab[:, 0:HALF], feature_half(fh, 0))
    logits[...] += dot(tab[:, HALF:D], feature_half(fh, 1))

    peak = jnp.max(logits[...], axis=0, keepdims=True)
    st_cur[0] = jnp.zeros((8, TOK), F32)
    st_cur[0, 0:1, :] = peak
    st_cur[0, 1:2, :] = jnp.sum(jnp.exp(logits[...] - peak), axis=0, keepdims=True)
    ar_start(1, st_cur, st_slot, 0)

    def stats_step(phase):
        ar_wait(1, st_cur, st_slot, phase)
        peaks = [st_cur[phase, 0:1, :]] + [st_slot[s, 0:1, :] for s, _ in ar_peers(phase)]
        sums = [st_cur[phase, 1:2, :]] + [st_slot[s, 1:2, :] for s, _ in ar_peers(phase)]
        top = peaks[0]
        for other in peaks[1:]:
            top = jnp.maximum(top, other)
        total = jnp.zeros_like(top)
        for a, b in zip(peaks, sums):
            total = total + b * jnp.exp(a - top)
        st_cur[phase + 1] = jnp.zeros((8, TOK), F32)
        st_cur[phase + 1, 0:1, :] = top
        st_cur[phase + 1, 1:2, :] = total
        if phase < 3:
            ar_start(1, st_cur, st_slot, phase + 1)

    stats_step(0)
    for s in range(PARTS):
        ag_second(1, xb, given, s)
    ar_sum(0, sm_cur, sm_slot, 0)
    ar_start(0, sm_cur, sm_slot, 1)
    stats_step(1)
    stats_step(2)
    ag_drain(0, fh)
    stats_step(3)

    top = st_cur[4, 0:1, :]
    scale = 1.0 / st_cur[4, 1:2, :]
    hot = jnp.where(tgt[...] == columns, 1.0, 0.0)
    grad = jnp.exp(logits[...] - top) * scale - hot
    logits[...] = grad
    gradt[...] = grad.T.astype(BF)

    def head_step(b, carry):
        k0 = pl.multiple_of(b * HB, HB)
        k1 = pl.multiple_of(D + b * HB, 16)
        block = dot(gradt[...], tab[:, pl.ds(k0, HB)]).T.astype(BF)
        fh[pl.ds(k0, HB), :] = block[:, 0:SEQ]
        fh[pl.ds(k1, HB), :] = block[:, SEQ:TOK]
        return carry

    steps = PART // HB
    for s in range(PARTS):
        lax.fori_loop(s * steps, (s + 1) * steps, head_step, 0)
        rs_sibling(0, fh, s)
        if s:
            rs_first(0, fh, s - 1)
    rs_first(0, fh, PARTS - 1)

    ar_sum(0, sm_cur, sm_slot, 1)
    ar_start(0, sm_cur, sm_slot, 2)
    for s in range(PARTS):
        ag_third(1, xb, given, s)
    for s in range(PARTS):
        ag_last(1, xb, given, s)
    hidden = dot(wupt[:, 0:HALF], feature_half(xb, 0)) + dot(wupt[:, HALF:D], feature_half(xb, 1))
    gate = jax.nn.sigmoid(hidden)
    slope[...] = gate * (1.0 + hidden * (1.0 - gate))
    inproj[...] = dot(pin[...], (hidden * gate).astype(BF))
    ar_sum(0, sm_cur, sm_slot, 2)
    ar_start(0, sm_cur, sm_slot, 3)

    def own_rows(k, s):
        return pl.ds(k * ROWS + s * SUB, SUB)

    def head_done(s):
        total = rs_third(0, s)

        @pl.when(sec == 3)
        def _():
            own[own_rows(0, s), :] = total

        @pl.when(sec != 3)
        def _():
            zr[own_rows(3, s), :] = total.astype(BF)
            rc(
                zr.at[own_rows(3, s)], zr.at[span(sec * ROWS + s * SUB, SUB)], z_send, z_recv.at[s, sec],
                dev(x, y, c, 3),
            ).start()

    def begin_last(s):
        total = own[own_rows(0, s), :]
        for z in range(3):
            held = zr.at[own_rows(z, s)]
            rc(held, held, z_send, z_recv.at[s, z], sib).wait_recv()
            total = total + zr[own_rows(z, s), :].astype(F32)
        cot[chained(x, y, c, s), :] = total.astype(BF)
        ag_first(2, cot, chained, s)

    def begin(s):
        held = cot.at[chained(x, y, c, s)]
        rc(held, held, c_send, c_recv.at[s], sib).wait_recv()
        ag_first(2, cot, chained, s)

    rs_second(0, fh, 0)
    rs_second(0, fh, 1)
    head_done(0)
    rs_second(0, fh, 2)
    head_done(1)
    local[4].wait()
    ag_drain(1, xb)

    @pl.when(sec == 3)
    def _():
        begin_last(0)

    head_done(2)

    @pl.when(sec == 3)
    def _():
        begin_last(1)
        ag_second(2, cot, chained, 0)
        begin_last(2)

    @pl.when(sec != 3)
    def _():
        @pl.when(sec == 0)
        def _():
            for s in range(PARTS):
                ag_first(3, pdt, given, s)
            for s in range(PARTS):
                ag_second(3, pdt, given, s)
            for s in range(PARTS):
                ag_third(3, pdt, given, s)
            for s in range(PARTS):
                ag_last(3, pdt, given, s)
            upside[...] = dot(wupt[...], pdt[0:D, :]).T[0:RANK, :].astype(BF)

        begin(0)
        begin(1)
        ag_second(2, cot, chained, 0)
        begin(2)

    def down(s):
        right = jnp.concatenate(
            [cot[pl.ds(s * PART, PART), :], cot[pl.ds(D + s * PART, PART), :]], axis=1
        )
        return dot(wdn[:, s * PART:(s + 1) * PART], right)

    ag_second(2, cot, chained, 1)
    ag_third(2, cot, chained, 0)
    ag_second(2, cot, chained, 2)
    ag_last(2, cot, chained, 0)
    act[...] = down(0)
    ag_third(2, cot, chained, 1)
    ag_last(2, cot, chained, 1)
    act[...] += down(1)
    ag_third(2, cot, chained, 2)
    ag_last(2, cot, chained, 2)
    total_act = act[...] + down(2)
    hgrad[...] = (total_act * slope[...]).astype(BF)

    def back(s):
        block = dot(wup[s * PART:(s + 1) * PART, :], hgrad[...]).astype(BF)
        xb[pl.ds(s * PART, PART), :] = block[:, 0:SEQ]
        xb[pl.ds(D + s * PART, PART), :] = block[:, SEQ:TOK]

    def section_grads():
        outproj = dot(pout[:, 0:HALF], feature_half(cot, 0)) + dot(pout[:, HALF:D], feature_half(cot, 1))
        la_cur[0] = outer_pair(outproj, inproj[...])
        ar_start(2, la_cur, la_slot, 0)

    def table_part():
        vside[...] = dot(pvoc[...], logits[...].astype(BF))
        ar_sum(0, sm_cur, sm_slot, 3)
        ta_cur[0] = outer_pair(vside[...], sm_cur[4, 0:RANK, :].astype(F32))

    def relay_done(s):
        total = rs_third(1, s) + cot[chained(x, y, c, s), :].astype(F32)
        zr[own_rows(4, s), :] = total.astype(BF)
        rc(
            zr.at[own_rows(4, s)], cot.at[chained(x, y, c, s)], c_send, c_recv.at[s], dev(x, y, c, (sec + 3) % 4)
        ).start()

    @pl.when(sec != 0)
    def _():
        for s in range(PARTS):
            back(s)
            rs_sibling(1, xb, s)
            if s:
                rs_first(1, xb, s - 1)
        rs_first(1, xb, PARTS - 1)
        section_grads()
        rs_second(1, xb, 0)
        rs_second(1, xb, 1)
        relay_done(0)
        rs_second(1, xb, 2)
        relay_done(1)
        relay_done(2)
        table_part()

    @pl.when(sec == 0)
    def _():
        table_part()
        embed = dot(upside[...], hgrad[...])
        for r in range(2):
            side = embed[:, r * SEQ:(r + 1) * SEQ]
            for s in range(PARTS):
                here = span(chain_start(x, y, c, s) - dp * D, SUB)
                term = dot(pdt[here, :], cot[chained(x, y, c, s), :], ((0,), (0,)))[0:RANK, :]
                side = side + jnp.where(dp == r, term, jnp.zeros_like(term))
            token = sm_cur[4, RANK:2 * RANK, r * SEQ:(r + 1) * SEQ].astype(F32)
            ta_cur[0, :, r * RANK:(r + 1) * RANK] += math.sqrt(D) * dot(
                token, side, ((1,), (1,)), lax.Precision.HIGHEST
            )

    ar_start(3, ta_cur, ta_slot, 0)

    @pl.when(sec == 0)
    def _():
        section_grads()

    for phase in range(3):
        ar_sum(3, ta_cur, ta_slot, phase)
        ar_start(3, ta_cur, ta_slot, phase + 1)
        ar_sum(2, la_cur, la_slot, phase)
        if phase < 2:
            ar_start(2, la_cur, la_slot, phase + 1)
    lay_out[...] = jnp.where(dp == 0, la_cur[3, :, 0:RANK], la_cur[3, :, RANK:2 * RANK])

    ag_drain(2, cot)
    rs_drain(0, fh)
    ar_drain(0, sm_slot, 10)
    ar_drain(1, st_slot, 10)
    ar_drain(2, la_slot, 7)

    @pl.when(sec != 3)
    def _():
        rc(piece(zr, 3), piece(zr, 3), z_send, z_recv.at[0, 0], sib).wait_send()

    @pl.when(sec != 0)
    def _():
        rc(piece(zr, 4), piece(zr, 4), c_send, c_recv.at[0], sib).wait_send()
        rs_drain(1, xb)

    @pl.when(sec == 0)
    def _():
        ag_drain(3, pdt)

    ar_sum(3, ta_cur, ta_slot, 3)
    tab_out[...] = jnp.where(dp == 0, ta_cur[4, :, 0:RANK], ta_cur[4, :, RANK:2 * RANK])
    ar_drain(3, ta_slot, 10)


def shards(x_in, final_hidden, w_up, w_down, table, token_ids, targets, proj_in, proj_out, proj_vocab, proj_dim):
    vmem = pl.BlockSpec(memory_space=pltpu.VMEM)
    hbm = pl.BlockSpec(memory_space=pl.ANY)
    full = lambda n: pltpu.VMEM((n * ROWS, SEQ), BF)
    dma = pltpu.SemaphoreType.DMA
    layer, tab = pl.pallas_call(
        kernel,
        out_shape=[jax.ShapeDtypeStruct((RANK, RANK), F32)] * 2,
        in_specs=[hbm] * 5 + [vmem] * 6,
        out_specs=[vmem] * 2,
        scratch_shapes=[
            pltpu.VMEM((VROWS, D), BF),
            pltpu.VMEM((UNITS, D), BF),
            pltpu.VMEM((D, UNITS), BF),
            pltpu.VMEM((UNITS, D), BF),
            full(32), full(32), full(32), full(32),
            full(2 * 16), full(2 * 12), full(2 * 3), full(5),
            pltpu.VMEM((VROWS, TOK), F32),
            pltpu.VMEM((TOK, VROWS), BF),
            pltpu.VMEM((UNITS, TOK), F32),
            pltpu.VMEM((UNITS, TOK), F32),
            pltpu.VMEM((UNITS, TOK), BF),
            pltpu.VMEM((RANK, TOK), F32),
            pltpu.VMEM((RANK, TOK), F32),
            pltpu.VMEM((RANK, UNITS), BF),
            pltpu.VMEM((ROWS, SEQ), F32),
            pltpu.VMEM((4 * ROWS, SEQ), F32),
            pltpu.VMEM((5, 2 * RANK, TOK), BF),
            pltpu.VMEM((10, 2 * RANK, TOK), BF),
            pltpu.VMEM((5, 8, TOK), F32),
            pltpu.VMEM((10, 8, TOK), F32),
            pltpu.VMEM((5, RANK, 2 * RANK), F32),
            pltpu.VMEM((10, RANK, 2 * RANK), F32),
            pltpu.VMEM((5, RANK, 2 * RANK), F32),
            pltpu.VMEM((10, RANK, 2 * RANK), F32),
            dma((5,)),
            dma((4,)), dma((4, PARTS, 32)),
            dma((2,)), dma((2, 11 * PARTS)),
            dma(()), dma((PARTS, 3)),
            dma(()), dma((PARTS,)),
            dma((4,)), dma((4, 10)),
        ],
        compiler_params=pltpu.CompilerParams(
            collective_id=0, has_side_effects=True, vmem_limit_bytes=62 * 1024 * 1024
        ),
    )(
        x_in[0], final_hidden, jnp.swapaxes(w_up[0], 0, 1), w_down[0], table,
        token_ids.reshape(1, TOK), targets.reshape(1, TOK),
        proj_in[0], proj_out[0], proj_vocab, proj_dim,
    )
    return layer[None, None], tab[None]


def solution(mesh):
    placed = (
        P("section", "tensor", "dp"),
        P("tensor", "dp"),
        P("section", None, ("tensor", "dp")),
        P("section", ("tensor", "dp"), None),
        P(("section", "tensor", "dp"), None),
        P(),
        P(),
        P("section", None, ("tensor", "dp")),
        P("section", None, None),
        P(None, ("section", "tensor", "dp")),
        P(None, "tensor"),
    )
    return jax.shard_map(
        shards,
        mesh=mesh,
        in_specs=placed,
        out_specs=(P("section", "dp", None, None), P("dp", None, None)),
        check_vma=False,
    )
```

time: 276 us -> 199 us (0.72)
  Pallas kernels: 261 us -> 196 us
  local copies, waits for them, and re-layouts: 14.1 us -> 2.75 us
    pallas_call x1, Pallas kernels: 261 us -> 196 us  [shards(): pl.pallas_call(kernel, out_shape=[jax.ShapeDtypeStruct((RANK, RANK), F32)...]
    unnamed x3 -> x2, local copies, waits for them, and re-layouts: 14.1 us -> 2.75 us
where the time goes in v2:
time: 199 us
  Pallas kernels  196 us (98%)
  local copies, waits for them, and re-layouts  2.75 us (1%)
    pallas_call x1, Pallas kernels, shards(): pl.pallas_call(kernel, out_shape=[jax.ShapeDtypeStruct((RANK, RANK), F32)...  196 us

profile of v2, /device:TPU:32, one launch (start us, length us, event | category | flops | bytes accessed | tf_op | source)
XLA Modules:
  0.0 199.0 jit_solution(9697993288686506157)
XLA Ops:
  0.6 195.6 %shard_map.122 = (f32[64,64]{1,0:T(8,128)}, f32[64,64]{1,0:T(8,128)}) custom-call(bf16[336,128]{1,0:T(8,128)(2,1)} %bitcast.15, bf16[336,128]{1,0:T(8,128)(2,1)} %fh_hbm.1, bf16[672,5376]{1,0:T(8,128)(2,1)} %bitcast.11, bf16[672,5376]{1,0:T(8,128)(2,1)} %bitcast.12, bf16[1024,5376]{1,0:T(8,128)(2,1)} %tab_hbm.1, s32[1,256]{1,0:T(1,128)} %bitcast.18, ...), custom_call_target="tpu_custom_call" | custom-call | tf_op jit(solution)/shard_map/pallas_call | solution.py:542
  196.2 1.4 copy.15
  197.6 1.4 copy.16

commit v3 on v2

--- a/solution.py
+++ b/solution.py
@@ -18,6 +18,7 @@
 SUB = ROWS // PARTS
 PART = D // PARTS
 HALF = D // 2
+FOLD = RANK // 2
 TB = 384
 HB = 896
 BF = jnp.bfloat16
@@ -30,10 +31,14 @@
 
 def outer_pair(left, right):
     parts = [
-        dot(left[:, q * SEQ:(q + 1) * SEQ], right[:, q * SEQ:(q + 1) * SEQ], ((1,), (1,)), lax.Precision.HIGHEST)
+        fold(dot(left[:, q * SEQ:(q + 1) * SEQ], right[:, q * SEQ:(q + 1) * SEQ], ((1,), (1,)), lax.Precision.HIGHEST))
         for q in range(2)
     ]
-    return jnp.concatenate(parts, axis=1)
+    return jnp.concatenate(parts, axis=0)
+
+
+def fold(square):
+    return jnp.concatenate([square[0:FOLD, :], square[FOLD:RANK, :]], axis=1)
 
 
 def kernel(
@@ -106,6 +111,8 @@
         partners.append(dev((x + k) % 4, y, c, sec))
         partners.append(dev(x, (y + k) % 4, c, sec))
         partners.append(dev(x, y, c, (sec + k) % 4))
+        for j in range(1, 4):
+            partners.append(dev((x + j) % 4, (y + k) % 4, c, sec))
     for partner in partners:
         pl.semaphore_signal(barrier, inc=1, device_id=partner, device_id_type=pl.DeviceIdType.MESH)
     pl.semaphore_wait(barrier, len(partners))
@@ -162,7 +169,7 @@
             start = ((n * PARTS + s) * 2 + r) * 8 * SUB
             rs_copy(n, src, r0, start, 8 * SUB, s * 11 + r, sib, r * D + s * PART + (1 - c) * 8 * SUB).start()
 
-    def pair_start(ka, u, s):
+    def run_start(ka, u, s):
         aa = (x * (1 - c) + y * c + ka) % 4
         return chain_start(aa * (1 - c) + 2 * u * c, aa * c + 2 * u * (1 - c), c, s)
 
@@ -177,12 +184,12 @@
                 start = ((n * PARTS + s) * 3 + ka - 1) * 4 * SUB + u * 2 * SUB
                 rs_copy(
                     n, src, r1, start, 2 * SUB, s * 11 + 2 + (ka - 1) * 2 + u, dev(*at(ka, 0), c, sec),
-                    pair_start(ka, u, s),
+                    run_start(ka, u, s),
                 ).start()
 
     def rs_second(n, src, s):
         for u in range(2):
-            here = span(pair_start(0, u, s), 2 * SUB)
+            here = span(run_start(0, u, s), 2 * SUB)
             total = src[here, :].astype(F32)
             for k in range(3):
                 start = ((n * PARTS + s) * 3 + k) * 4 * SUB + u * 2 * SUB
@@ -239,6 +246,44 @@
             total = total + slot[s].astype(F32)
         cur[phase + 1] = total.astype(cur.dtype)
 
+    def pair_copies(n, cur, slot, phase):
+        copies = []
+        for s, device in ar_peers(phase):
+            if phase == 0:
+                src, dst = cur.at[0], slot.at[0]
+            elif phase == 1:
+                src = cur.at[1, pl.ds(pl.multiple_of(((x + s) % 4) // 2 * FOLD, FOLD), FOLD)]
+                dst = slot.at[s, pl.ds(0, FOLD)]
+            else:
+                src, dst = cur.at[phase, pl.ds(0, FOLD)], slot.at[s, pl.ds(0, FOLD)]
+            copies.append(rc(src, dst, ar_send.at[n], ar_recv.at[n, s], device))
+        return copies
+
+    def pair_start(n, cur, slot, phase):
+        for copy in pair_copies(n, cur, slot, phase):
+            copy.start()
+
+    def pair_sum(n, cur, slot, phase):
+        for copy in pair_copies(n, cur, slot, phase):
+            copy.wait_recv()
+        if phase == 0:
+            cur[1] = cur[0] + slot[0]
+            return
+        total = cur[1, pl.ds(pl.multiple_of(dp * FOLD, FOLD), FOLD), :] if phase == 1 else cur[phase, 0:FOLD, :]
+        for s, _ in ar_peers(phase):
+            total = total + slot[s, 0:FOLD, :]
+        cur[phase + 1, 0:FOLD, :] = total
+
+    def pair_drain(n, slot, count):
+        part = slot.at[pl.ds(0, 1)]
+        rc(part, part, ar_send.at[n], ar_recv.at[n, 0], sib).wait_send()
+        part = slot.at[pl.ds(1, count), pl.ds(0, FOLD)]
+        rc(part, part, ar_send.at[n], ar_recv.at[n, 0], sib).wait_send()
+
+    def unfold(out, cur, phase):
+        out[0:FOLD, :] = cur[phase, 0:FOLD, 0:RANK]
+        out[FOLD:RANK, :] = cur[phase, 0:FOLD, RANK:2 * RANK]
+
     def ar_drain(n, slot, count):
         part = slot.at[pl.ds(0, count)]
         rc(part, part, ar_send.at[n], ar_recv.at[n, 0], sib).wait_send()
@@ -288,12 +333,27 @@
     st_cur[0] = jnp.zeros((8, TOK), F32)
     st_cur[0, 0:1, :] = peak
     st_cur[0, 1:2, :] = jnp.sum(jnp.exp(logits[...] - peak), axis=0, keepdims=True)
-    ar_start(1, st_cur, st_slot, 0)
+
+    def stats_peers(phase):
+        if phase == 0:
+            return [(0, sib)]
+        if phase == 1:
+            return [
+                (4 * i + j, dev((x + i) % 4, (y + j) % 4, c, sec)) for i in (2, 1, 3, 0) for j in (2, 1, 3, 0) if i or j
+            ]
+        return [(15 + k, dev(x, y, c, (sec + k) % 4)) for k in (2, 1, 3)]
+
+    def stats_copies(phase):
+        return [
+            rc(st_cur.at[phase], st_slot.at[s], ar_send.at[1], ar_recv.at[1, s], device)
+            for s, device in stats_peers(phase)
+        ]
 
     def stats_step(phase):
-        ar_wait(1, st_cur, st_slot, phase)
-        peaks = [st_cur[phase, 0:1, :]] + [st_slot[s, 0:1, :] for s, _ in ar_peers(phase)]
-        sums = [st_cur[phase, 1:2, :]] + [st_slot[s, 1:2, :] for s, _ in ar_peers(phase)]
+        for copy in stats_copies(phase):
+            copy.wait_recv()
+        peaks = [st_cur[phase, 0:1, :]] + [st_slot[s, 0:1, :] for s, _ in stats_peers(phase)]
+        sums = [st_cur[phase, 1:2, :]] + [st_slot[s, 1:2, :] for s, _ in stats_peers(phase)]
         top = peaks[0]
         for other in peaks[1:]:
             top = jnp.maximum(top, other)
@@ -303,21 +363,23 @@
         st_cur[phase + 1] = jnp.zeros((8, TOK), F32)
         st_cur[phase + 1, 0:1, :] = top
         st_cur[phase + 1, 1:2, :] = total
-        if phase < 3:
-            ar_start(1, st_cur, st_slot, phase + 1)
-
+        if phase < 2:
+            for copy in stats_copies(phase + 1):
+                copy.start()
+
+    for copy in stats_copies(0):
+        copy.start()
     stats_step(0)
     for s in range(PARTS):
         ag_second(1, xb, given, s)
     ar_sum(0, sm_cur, sm_slot, 0)
     ar_start(0, sm_cur, sm_slot, 1)
     stats_step(1)
+    ag_drain(0, fh)
     stats_step(2)
-    ag_drain(0, fh)
-    stats_step(3)
-
-    top = st_cur[4, 0:1, :]
-    scale = 1.0 / st_cur[4, 1:2, :]
+
+    top = st_cur[3, 0:1, :]
+    scale = 1.0 / st_cur[3, 1:2, :]
     hot = jnp.where(tgt[...] == columns, 1.0, 0.0)
     grad = jnp.exp(logits[...] - top) * scale - hot
     logits[...] = grad
@@ -423,23 +485,26 @@
         ag_second(2, cot, chained, 0)
         begin(2)
 
-    def down(s):
-        right = jnp.concatenate(
-            [cot[pl.ds(s * PART, PART), :], cot[pl.ds(D + s * PART, PART), :]], axis=1
-        )
-        return dot(wdn[:, s * PART:(s + 1) * PART], right)
+    def down(s, cc):
+        k0 = pl.multiple_of(s * PART + cc * (PART // 2), 128)
+        k1 = pl.multiple_of(D + s * PART + cc * (PART // 2), 16)
+        right = jnp.concatenate([cot[pl.ds(k0, PART // 2), :], cot[pl.ds(k1, PART // 2), :]], axis=1)
+        return dot(wdn[:, pl.ds(k0, PART // 2)], right)
 
     ag_second(2, cot, chained, 1)
     ag_third(2, cot, chained, 0)
     ag_second(2, cot, chained, 2)
+    act[...] = down(0, c)
     ag_last(2, cot, chained, 0)
-    act[...] = down(0)
+    act[...] += down(0, 1 - c)
     ag_third(2, cot, chained, 1)
+    act[...] += down(1, c)
     ag_last(2, cot, chained, 1)
-    act[...] += down(1)
+    act[...] += down(1, 1 - c)
     ag_third(2, cot, chained, 2)
+    act[...] += down(2, c)
     ag_last(2, cot, chained, 2)
-    total_act = act[...] + down(2)
+    total_act = act[...] + down(2, 1 - c)
     hgrad[...] = (total_act * slope[...]).astype(BF)
 
     def back(s):
@@ -450,7 +515,7 @@
     def section_grads():
         outproj = dot(pout[:, 0:HALF], feature_half(cot, 0)) + dot(pout[:, HALF:D], feature_half(cot, 1))
         la_cur[0] = outer_pair(outproj, inproj[...])
-        ar_start(2, la_cur, la_slot, 0)
+        pair_start(2, la_cur, la_slot, 0)
 
     def table_part():
         vside[...] = dot(pvoc[...], logits[...].astype(BF))
@@ -492,29 +557,29 @@
                 term = dot(pdt[here, :], cot[chained(x, y, c, s), :], ((0,), (0,)))[0:RANK, :]
                 side = side + jnp.where(dp == r, term, jnp.zeros_like(term))
             token = sm_cur[4, RANK:2 * RANK, r * SEQ:(r + 1) * SEQ].astype(F32)
-            ta_cur[0, :, r * RANK:(r + 1) * RANK] += math.sqrt(D) * dot(
-                token, side, ((1,), (1,)), lax.Precision.HIGHEST
+            ta_cur[0, r * FOLD:(r + 1) * FOLD, :] += math.sqrt(D) * fold(
+                dot(token, side, ((1,), (1,)), lax.Precision.HIGHEST)
             )
 
-    ar_start(3, ta_cur, ta_slot, 0)
+    pair_start(3, ta_cur, ta_slot, 0)
 
     @pl.when(sec == 0)
     def _():
         section_grads()
 
     for phase in range(3):
-        ar_sum(3, ta_cur, ta_slot, phase)
-        ar_start(3, ta_cur, ta_slot, phase + 1)
-        ar_sum(2, la_cur, la_slot, phase)
+        pair_sum(3, ta_cur, ta_slot, phase)
+        pair_start(3, ta_cur, ta_slot, phase + 1)
+        pair_sum(2, la_cur, la_slot, phase)
         if phase < 2:
-            ar_start(2, la_cur, la_slot, phase + 1)
-    lay_out[...] = jnp.where(dp == 0, la_cur[3, :, 0:RANK], la_cur[3, :, RANK:2 * RANK])
+            pair_start(2, la_cur, la_slot, phase + 1)
+    unfold(lay_out, la_cur, 3)
 
     ag_drain(2, cot)
     rs_drain(0, fh)
     ar_drain(0, sm_slot, 10)
-    ar_drain(1, st_slot, 10)
-    ar_drain(2, la_slot, 7)
+    ar_drain(1, st_slot, 19)
+    pair_drain(2, la_slot, 6)
 
     @pl.when(sec != 3)
     def _():
@@ -529,9 +594,9 @@
     def _():
         ag_drain(3, pdt)
 
-    ar_sum(3, ta_cur, ta_slot, 3)
-    tab_out[...] = jnp.where(dp == 0, ta_cur[4, :, 0:RANK], ta_cur[4, :, RANK:2 * RANK])
-    ar_drain(3, ta_slot, 10)
+    pair_sum(3, ta_cur, ta_slot, 3)
+    unfold(tab_out, ta_cur, 4)
+    pair_drain(3, ta_slot, 9)
 
 
 def shards(x_in, final_hidden, w_up, w_down, table, token_ids, targets, proj_in, proj_out, proj_vocab, proj_dim):
@@ -563,8 +628,8 @@
             pltpu.VMEM((4 * ROWS, SEQ), F32),
             pltpu.VMEM((5, 2 * RANK, TOK), BF),
             pltpu.VMEM((10, 2 * RANK, TOK), BF),
-            pltpu.VMEM((5, 8, TOK), F32),
-            pltpu.VMEM((10, 8, TOK), F32),
+            pltpu.VMEM((4, 8, TOK), F32),
+            pltpu.VMEM((19, 8, TOK), F32),
             pltpu.VMEM((5, RANK, 2 * RANK), F32),
             pltpu.VMEM((10, RANK, 2 * RANK), F32),
             pltpu.VMEM((5, RANK, 2 * RANK), F32),
@@ -574,7 +639,7 @@
             dma((2,)), dma((2, 11 * PARTS)),
             dma(()), dma((PARTS, 3)),
             dma(()), dma((PARTS,)),
-            dma((4,)), dma((4, 10)),
+            dma((4,)), dma((4, 19)),
         ],
         compiler_params=pltpu.CompilerParams(
             collective_id=0, has_side_effects=True, vmem_limit_bytes=62 * 1024 * 1024

time: 199 us -> 191 us (0.960)
  Pallas kernels: 196 us -> 187 us
    pallas_call x1, Pallas kernels: 196 us -> 187 us  [shards(): pl.pallas_call(kernel, out_shape=[jax.ShapeDtypeStruct((RANK, RANK), F32)...]
where the time goes in v3:
time: 191 us
  Pallas kernels  187 us (98%)
  local copies, waits for them, and re-layouts  2.75 us (1%)
    pallas_call x1, Pallas kernels, shards(): pl.pallas_call(kernel, out_shape=[jax.ShapeDtypeStruct((RANK, RANK), F32)...  187 us

profile of v3, /device:TPU:32, one launch (start us, length us, event | category | flops | bytes accessed | tf_op | source)
XLA Modules:
  0.0 190.8 jit_solution(15806506736580988191)
XLA Ops:
  0.6 187.4 %shard_map.122 = (f32[64,64]{1,0:T(8,128)}, f32[64,64]{1,0:T(8,128)}) custom-call(bf16[336,128]{1,0:T(8,128)(2,1)} %bitcast.15, bf16[336,128]{1,0:T(8,128)(2,1)} %fh_hbm.1, bf16[672,5376]{1,0:T(8,128)(2,1)} %bitcast.11, bf16[672,5376]{1,0:T(8,128)(2,1)} %bitcast.12, bf16[1024,5376]{1,0:T(8,128)(2,1)} %tab_hbm.1, s32[1,256]{1,0:T(1,128)} %bitcast.18, ...), custom_call_target="tpu_custom_call" | custom-call | tf_op jit(solution)/shard_map/pallas_call | solution.py:607
  188.1 1.4 copy.15
  189.5 1.4 copy.16

commit v4 on v3

--- a/solution.py
+++ b/solution.py
@@ -43,7 +43,7 @@
 
 def kernel(
     x_hbm, fh_hbm, wupt_hbm, wdn_hbm, tab_hbm, tok, tgt, pin, pout, pvoc, pdim,
-    lay_out, tab_out,
+    both_out,
     tab, wupt, wup, wdn, fh, xb, cot, pdt,
     r0, r1, r2, zr,
     logits, gradt, act, slope, hgrad, inproj, vside, upside, own, sums,
@@ -537,13 +537,13 @@
             if s:
                 rs_first(1, xb, s - 1)
         rs_first(1, xb, PARTS - 1)
-        section_grads()
         rs_second(1, xb, 0)
         rs_second(1, xb, 1)
         relay_done(0)
         rs_second(1, xb, 2)
         relay_done(1)
         relay_done(2)
+        section_grads()
         table_part()
 
     @pl.when(sec == 0)
@@ -573,7 +573,7 @@
         pair_sum(2, la_cur, la_slot, phase)
         if phase < 2:
             pair_start(2, la_cur, la_slot, phase + 1)
-    unfold(lay_out, la_cur, 3)
+    unfold(both_out.at[0], la_cur, 3)
 
     ag_drain(2, cot)
     rs_drain(0, fh)
@@ -595,7 +595,7 @@
         ag_drain(3, pdt)
 
     pair_sum(3, ta_cur, ta_slot, 3)
-    unfold(tab_out, ta_cur, 4)
+    unfold(both_out.at[1], ta_cur, 4)
     pair_drain(3, ta_slot, 9)
 
 
@@ -604,11 +604,11 @@
     hbm = pl.BlockSpec(memory_space=pl.ANY)
     full = lambda n: pltpu.VMEM((n * ROWS, SEQ), BF)
     dma = pltpu.SemaphoreType.DMA
-    layer, tab = pl.pallas_call(
+    both = pl.pallas_call(
         kernel,
-        out_shape=[jax.ShapeDtypeStruct((RANK, RANK), F32)] * 2,
+        out_shape=jax.ShapeDtypeStruct((2, RANK, RANK), F32),
         in_specs=[hbm] * 5 + [vmem] * 6,
-        out_specs=[vmem] * 2,
+        out_specs=vmem,
         scratch_shapes=[
             pltpu.VMEM((VROWS, D), BF),
             pltpu.VMEM((UNITS, D), BF),
@@ -649,7 +649,7 @@
         token_ids.reshape(1, TOK), targets.reshape(1, TOK),
         proj_in[0], proj_out[0], proj_vocab, proj_dim,
     )
-    return layer[None, None], tab[None]
+    return both[0][None, None], both[1][None]
 
 
 def solution(mesh):

time: 191 us -> 190 us (level)
    unnamed x2 -> x0, local copies, waits for them, and re-layouts: 2.75 us -> none
where the time goes in v4:
time: 190 us; the launch traced here: 189 us
  Pallas kernels  187 us (98%)
    pallas_call x1, Pallas kernels, shards(): pl.pallas_call(kernel, out_shape=jax.ShapeDtypeStruct((2, RANK, RANK), F3...  187 us

profile of v4, /device:TPU:32, one launch (start us, length us, event | category | flops | bytes accessed | tf_op | source)
XLA Modules:
  0.0 189.4 jit_solution(8485850977706978476)
XLA Ops:
  0.6 187.4 %shard_map.122 = f32[2,64,64]{2,1,0:T(8,128)} custom-call(bf16[336,128]{1,0:T(8,128)(2,1)} %bitcast.15, bf16[336,128]{1,0:T(8,128)(2,1)} %fh_hbm.1, bf16[672,5376]{1,0:T(8,128)(2,1)} %bitcast.11, bf16[672,5376]{1,0:T(8,128)(2,1)} %bitcast.12, bf16[1024,5376]{1,0:T(8,128)(2,1)} %tab_hbm.1, s32[1,256]{1,0:T(1,128)} %bitcast.16, s32[1,256]{1,0:T(1,128)} %bitcast.17, ...), custom_call_target="tpu_custom_call" | custom-call | tf_op jit(solution)/shard_map/pallas_call | solution.py:607
  188.0 1.4 fusion

commit v5 on v4

--- a/solution.py
+++ b/solution.py
@@ -446,6 +446,11 @@
         rc(held, held, c_send, c_recv.at[s], sib).wait_recv()
         ag_first(2, cot, chained, s)
 
+    def table_part():
+        vside[...] = dot(pvoc[...], logits[...].astype(BF))
+        ar_sum(0, sm_cur, sm_slot, 3)
+        ta_cur[0] = outer_pair(vside[...], sm_cur[4, 0:RANK, :].astype(F32))
+
     rs_second(0, fh, 0)
     rs_second(0, fh, 1)
     head_done(0)
@@ -479,6 +484,7 @@
             for s in range(PARTS):
                 ag_last(3, pdt, given, s)
             upside[...] = dot(wupt[...], pdt[0:D, :]).T[0:RANK, :].astype(BF)
+            table_part()
 
         begin(0)
         begin(1)
@@ -517,11 +523,6 @@
         la_cur[0] = outer_pair(outproj, inproj[...])
         pair_start(2, la_cur, la_slot, 0)
 
-    def table_part():
-        vside[...] = dot(pvoc[...], logits[...].astype(BF))
-        ar_sum(0, sm_cur, sm_slot, 3)
-        ta_cur[0] = outer_pair(vside[...], sm_cur[4, 0:RANK, :].astype(F32))
-
     def relay_done(s):
         total = rs_third(1, s) + cot[chained(x, y, c, s), :].astype(F32)
         zr[own_rows(4, s), :] = total.astype(BF)
@@ -548,14 +549,13 @@
 
     @pl.when(sec == 0)
     def _():
-        table_part()
         embed = dot(upside[...], hgrad[...])
+        term = jnp.zeros((RANK, SEQ), F32)
+        for s in range(PARTS):
+            here = span(chain_start(x, y, c, s) - dp * D, SUB)
+            term = term + dot(pdt[here, :], cot[chained(x, y, c, s), :], ((0,), (0,)))[0:RANK, :]
         for r in range(2):
-            side = embed[:, r * SEQ:(r + 1) * SEQ]
-            for s in range(PARTS):
-                here = span(chain_start(x, y, c, s) - dp * D, SUB)
-                term = dot(pdt[here, :], cot[chained(x, y, c, s), :], ((0,), (0,)))[0:RANK, :]
-                side = side + jnp.where(dp == r, term, jnp.zeros_like(term))
+            side = embed[:, r * SEQ:(r + 1) * SEQ] + jnp.where(dp == r, term, jnp.zeros_like(term))
             token = sm_cur[4, RANK:2 * RANK, r * SEQ:(r + 1) * SEQ].astype(F32)
             ta_cur[0, r * FOLD:(r + 1) * FOLD, :] += math.sqrt(D) * fold(
                 dot(token, side, ((1,), (1,)), lax.Precision.HIGHEST)
@@ -563,13 +563,17 @@
 
     pair_start(3, ta_cur, ta_slot, 0)
 
+    pair_sum(3, ta_cur, ta_slot, 0)
+    pair_start(3, ta_cur, ta_slot, 1)
+
     @pl.when(sec == 0)
     def _():
         section_grads()
 
     for phase in range(3):
-        pair_sum(3, ta_cur, ta_slot, phase)
-        pair_start(3, ta_cur, ta_slot, phase + 1)
+        if phase:
+            pair_sum(3, ta_cur, ta_slot, phase)
+            pair_start(3, ta_cur, ta_slot, phase + 1)
         pair_sum(2, la_cur, la_slot, phase)
         if phase < 2:
             pair_start(2, la_cur, la_slot, phase + 1)

time: 190 us -> 190 us (level)
  no operation moved by 1% of the time
where the time goes in v5:
time: 190 us; the launch traced here: 189 us
  Pallas kernels  187 us (98%)
    pallas_call x1, Pallas kernels, shards(): pl.pallas_call(kernel, out_shape=jax.ShapeDtypeStruct((2, RANK, RANK), F3...  187 us

profile of v5, /device:TPU:32, one launch (start us, length us, event | category | flops | bytes accessed | tf_op | source)
XLA Modules:
  0.0 189.0 jit_solution(15154340628778393642)
XLA Ops:
  0.6 186.9 %shard_map.122 = f32[2,64,64]{2,1,0:T(8,128)} custom-call(bf16[336,128]{1,0:T(8,128)(2,1)} %bitcast.15, bf16[336,128]{1,0:T(8,128)(2,1)} %fh_hbm.1, bf16[672,5376]{1,0:T(8,128)(2,1)} %bitcast.11, bf16[672,5376]{1,0:T(8,128)(2,1)} %bitcast.12, bf16[1024,5376]{1,0:T(8,128)(2,1)} %tab_hbm.1, s32[1,256]{1,0:T(1,128)} %bitcast.16, s32[1,256]{1,0:T(1,128)} %bitcast.17, ...), custom_call_target="tpu_custom_call" | custom-call | tf_op jit(solution)/shard_map/pallas_call | solution.py:611
  187.6 1.4 fusion
